TPU v7x, 32 devices: a whole 2x2x4 slice. The times are simulated.
32 devices in a mesh: tgt: 8 (over z, x), band: 4 (over y, core).
Axes of the slice: x: 2, y: 2, z: 4, core: 2. Of those that a mesh axis runs over, the one named last changes fastest.
Arguments:
- exposure_flux: bfloat16 [1024, 4096], P('tgt', 'band'), may hold values from -6 to 6
- exposure_ivar: bfloat16 [1024, 4096], P('tgt', 'band'), may hold values from 0.19921875 to 5
- exposure_res: bfloat16 [1024, 11, 4096], P('tgt', None, 'band'), may hold values from 0 to 1
- target_of_row: int32 [1024], replicated, may hold values from 0 to 127, as said below
- valid_of_row: int32 [1024], replicated, may hold values from 0 to 1, as said below
- rest_basis: float32 [10, 4608], replicated, may hold values from -6 to 6
- redshift_shift: int32 [32], replicated, may hold values from 0 to 511
Outputs:
- coadd_flux: float32 [128, 4096], P('tgt', 'band')
- coadd_res: bfloat16 [128, 11, 4096], P('tgt', None, 'band')
- fit_gain: float32 [128, 32], P('tgt', 'band')
Inputs may be any that keep to these rules, and one draw needn't show every extreme that they name: `target_of_row`: every target has exactly 8 rows. The rows held by one index of tgt (rows j * 128 to (j + 1) * 128 - 1) include at most 32 rows of the targets of any one owner, where the owner of target t is t // 16; some pairs reach 32. `valid_of_row`: every target has at least one row with flag 1.
All inputs are finite; a program needn't handle non-finite values.
Results may differ from a plain program's by a relative error of at most 0.004.
Values may be sent and summed in bfloat16 or wider, within the bound.
A program may use at most 128 MiB of HBM per device.

v0:
```python
import jax
import jax.numpy as jnp
import numpy as np
from jax import lax
from jax.sharding import PartitionSpec as P

TGT_DEV = 16
NDIAG = 11
Z_DEV = 8


pair_first, pair_second = np.triu_indices(10)


def solve_normal(matrix, right_side):
    basis_count = right_side.shape[0]
    rows_of = [[None] * basis_count for column in range(basis_count)]
    for p in range(len(pair_first)):
        b = int(pair_first[p])
        c = int(pair_second[p])
        rows_of[b][c] = matrix[p]
        rows_of[c][b] = matrix[p]
    vector = [right_side[b] for b in range(basis_count)]
    for k in range(basis_count):
        inverse = 1.0 / rows_of[k][k]
        for r in range(k + 1, basis_count):
            factor = rows_of[r][k] * inverse
            for c in range(k + 1, basis_count):
                rows_of[r][c] = rows_of[r][c] - factor * rows_of[k][c]
            vector[r] = vector[r] - factor * vector[k]
    answer = [None] * basis_count
    for k in reversed(range(basis_count)):
        running = vector[k]
        for c in range(k + 1, basis_count):
            running = running - rows_of[k][c] * answer[c]
        answer[k] = running / rows_of[k][k]
    gain_total = right_side[0] * answer[0]
    for b in range(1, basis_count):
        gain_total = gain_total + right_side[b] * answer[b]
    return gain_total


def basis_windows(rest_basis, shifts, first_wave, length):

    def one_shift(shift_value):
        return lax.dynamic_slice_in_dim(rest_basis, first_wave + shift_value, length, axis=1)

    return jax.vmap(one_shift)(shifts)


def normal_terms(weight_sum, flux_sum, windows):
    products = windows[:, pair_first, :] * windows[:, pair_second, :]
    matrix = jnp.einsum("ti,zpi->ztp", weight_sum, products, precision=lax.Precision.HIGHEST)
    right_side = jnp.einsum("ti,zbi->ztb", flux_sum, windows, precision=lax.Precision.HIGHEST)
    return (matrix, right_side)


def blocked_normals(weight_sum, flux_sum, rest_basis, shifts, first_wave, length):
    total_shifts = shifts.shape[0]
    block_size = 8
    grouped = shifts.reshape(total_shifts // block_size, block_size)

    def one_block(shift_block):
        return normal_terms(
            weight_sum, flux_sum, basis_windows(rest_basis, shift_block, first_wave, length)
        )

    matrix, right_side = lax.map(one_block, grouped)
    return (
        matrix.reshape((total_shifts,) + matrix.shape[2:]),
        right_side.reshape((total_shifts,) + right_side.shape[2:]),
    )


def fit_from(matrix, right_side):
    pairs = jnp.transpose(matrix, (2, 0, 1)).reshape(matrix.shape[2], -1)
    sides = jnp.transpose(right_side, (2, 0, 1)).reshape(right_side.shape[2], -1)
    gain = solve_normal(pairs, sides).reshape(matrix.shape[0], matrix.shape[1])
    return gain.T


def shards(
    exposure_flux,
    exposure_ivar,
    exposure_res,
    target_of_row,
    valid_of_row,
    rest_basis,
    redshift_shift,
):
    owners = lax.axis_size("tgt")
    device = lax.axis_index("tgt")
    row_count = exposure_flux.shape[0]
    wave_dev = exposure_flux.shape[1]
    capacity = 2 * row_count // owners
    own_target = lax.dynamic_slice_in_dim(target_of_row, device * row_count, row_count)
    owner_of = own_target // TGT_DEV
    row_ids = jnp.arange(row_count, dtype=jnp.int32)
    earlier = row_ids[None, :] < row_ids[:, None]
    position = jnp.sum(jnp.logical_and(owner_of[:, None] == owner_of[None, :], earlier), axis=1)
    slot_index = owner_of * capacity + position
    source_row = jnp.full((owners * capacity,), row_count, jnp.int32).at[slot_index].set(row_ids)

    def packed(values):
        gathered = jnp.take(values, source_row, axis=0, mode="fill", fill_value=0)
        return gathered.reshape((owners, capacity) + values.shape[1:])

    target_table = target_of_row.reshape(owners, row_count)
    is_mine = (target_table // TGT_DEV == device).astype(jnp.int32)
    before = jnp.cumsum(is_mine, axis=1) - is_mine
    matches = jnp.logical_and(
        is_mine[:, :, None] == 1,
        before[:, :, None] == jnp.arange(capacity, dtype=jnp.int32)[None, None, :],
    ).astype(jnp.int32)
    present = jnp.sum(matches, axis=1)
    local_target = jnp.sum(matches * (target_table % TGT_DEV)[:, :, None], axis=1)
    member = (
        jnp.logical_and(
            local_target[None] == jnp.arange(TGT_DEV, dtype=jnp.int32)[:, None, None],
            present[None] == 1,
        )
        .astype(jnp.float32)
        .reshape(TGT_DEV, owners * capacity)
    )
    outgoing = (packed(exposure_flux), packed(exposure_ivar), packed(exposure_res))
    got_flux, got_ivar, got_res = (
        lax.all_to_all(outgoing[0], "tgt", split_axis=0, concat_axis=0, tiled=True),
        lax.all_to_all(outgoing[1], "tgt", split_axis=0, concat_axis=0, tiled=True),
        lax.all_to_all(outgoing[2], "tgt", split_axis=0, concat_axis=0, tiled=True),
    )
    flag_table = valid_of_row.reshape(owners, row_count)
    usable = jnp.sum(matches * flag_table[:, :, None], axis=1)
    weight = got_ivar.astype(jnp.float32) * usable[:, :, None].astype(jnp.float32)
    flux_terms = weight * got_flux.astype(jnp.float32)
    res_terms = (weight[:, :, None, :] * got_res.astype(jnp.float32)).reshape(owners * capacity, -1)
    weight_sum = jnp.dot(
        member, weight.reshape(owners * capacity, wave_dev), precision=lax.Precision.HIGHEST
    )
    flux_sum = jnp.dot(
        member, flux_terms.reshape(owners * capacity, wave_dev), precision=lax.Precision.HIGHEST
    )
    res_sum = jnp.dot(member, res_terms, precision=lax.Precision.HIGHEST).reshape(
        TGT_DEV, NDIAG, wave_dev
    )
    coadd_flux = flux_sum / weight_sum
    coadd_res = (res_sum / weight_sum[:, None, :]).astype(jnp.bfloat16)
    band_index = lax.axis_index("band")
    weight_all, flux_all = (
        lax.all_gather(weight_sum.astype(jnp.bfloat16), "band", axis=1, tiled=True).astype(
            weight_sum.dtype
        ),
        lax.all_gather(flux_sum.astype(jnp.bfloat16), "band", axis=1, tiled=True).astype(
            flux_sum.dtype
        ),
    )
    shifts = lax.dynamic_slice_in_dim(redshift_shift, band_index * Z_DEV, Z_DEV)
    matrix, right_side = blocked_normals(
        weight_all, flux_all, rest_basis, shifts, 0, weight_all.shape[1]
    )
    fit_gain = fit_from(matrix, right_side)
    return (coadd_flux, coadd_res, fit_gain)


def solution(mesh):
    in_specs = (P("tgt", "band"), P("tgt", "band"), P("tgt", None, "band"), P(), P(), P(), P())
    out_specs = (P("tgt", "band"), P("tgt", None, "band"), P("tgt", "band"))
    return jax.shard_map(shards, mesh=mesh, in_specs=in_specs, out_specs=out_specs, check_vma=False)
```

profile of v0, /device:TPU:0, one launch (start us, length us, event | category | flops | bytes accessed | tf_op | source)
XLA Modules:
  0.0 265.6 jit_solution(9407625586820401071)
XLA Ops:
  0.6 0.0 copy-start
  0.7 0.9 and_select_fusion
  1.6 0.2 convert_reduce_fusion.1
  1.8 0.8 compare_select_fusion.2
  2.6 1.0 scatter_custom_fusion
  3.6 3.3 %gather_fusion.3 = bf16[256,1024]{1,0:T(8,128)(2,1)} fusion(bf16[128,1024]{1,0:T(8,128)(2,1)} %param.14, s32[1024]{0:T(1024)S(1)} %pad_clamp_fusion.2), kind=kCustom, calls=%fused_computation.clone | custom fusion | bytes 1049600 | tf_op jit(solution)/shard_map/jit(_take)/gather | solution.py:105
  6.9 2.0 gather_fusion.4
  8.9 2.1 broadcast_select_fusion.1
  11.0 21.6 %all_to_all.15 = bf16[8,32,1024]{2,1,0:T(8,128)(2,1)S(1)} all-to-all(bf16[8,32,1024]{2,1,0:T(8,128)(2,1)S(1)} %bitcast.401), channel_id=1, replica_groups=mesh['tgt'=8,'band'=4] {'tgt'}, dimensions={0} | all-to-all | bytes 1048576 | tf_op jit(solution)/shard_map/all_to_all | solution.py:128
  32.6 4.3 %all-to-all-start.1 = ((bf16[8,32,1024]{2,1,0:T(8,128)(2,1)}), bf16[8,32,1024]{2,1,0:T(8,128)(2,1)}, u32[]{:S(2)}, u32[]{:S(2)}) async-start(bf16[8,32,1024]{2,1,0:T(8,128)(2,1)} %bitcast.400), calls=%async_computation.1 | async-start | bytes 1048576 | tf_op jit(solution)/shard_map/all_to_all | solution.py:127
  36.9 0.1 broadcast_in_dim.65
  37.0 20.2 %gather_fusion = bf16[256,11,1024]{2,0,1:T(8,128)(2,1)} fusion(bf16[128,11,1024]{2,0,1:T(8,128)(2,1)S(1)} %copy-done, s32[1024]{0:T(1024)S(1)} %pad_clamp_fusion.2), kind=kCustom, calls=%fused_computation.2 | custom fusion | bytes 11535360 | tf_op jit(solution)/shard_map/jit(_take)/gather | solution.py:105
  57.2 5.6 %copy_select_fusion = bf16[8,32,11,1024]{3,1,2,0:T(8,128)(2,1)} fusion(bf16[8,32,11,1024]{3,1,0,2:T(8,128)(2,1)} %bitcast.399, pred[8,32]{1,0:T(8,128)(4,1)S(1)} %broadcast_in_dim.65), kind=kLoop, calls=%fused_computation.12 | loop fusion | flops 2883584 | bytes 11534592 | tf_op jit(solution)/shard_map/jit(_take)/select_n | solution.py:105
  62.8 0.0 copy-start.7
  62.8 0.0 all-to-all-done.1
  62.8 6.0 %all-to-all-start.2 = ((bf16[8,32,11,1024]{3,1,2,0:T(8,128)(2,1)}), bf16[8,32,11,1024]{3,1,2,0:T(8,128)(2,1)}, u32[]{:S(2)}, u32[]{:S(2)}) async-start(bf16[8,32,11,1024]{3,1,2,0:T(8,128)(2,1)} %copy_select_fusion), calls=%async_computation.2 | async-start | bytes 11534336 | tf_op jit(solution)/shard_map/all_to_all | solution.py:129
  68.9 0.3 reduce_window_sum.11
  69.2 0.5 convert_reduce_fusion
  69.7 0.1 fusion.94
  69.8 16.6 %while.1 = (s32[]{:T(128)}, f32[10,4608]{1,0:T(8,128)S(1)}, s32[8,2]{0,1:T(2,128)S(1)}, f32[8,10,4096]{2,1,0:T(8,128)}, s32[]{:T(128)}) while((s32[]{:T(128)}, f32[10,4608]{1,0:T(8,128)S(1)}, s32[8,2]{0,1:T(2,128)S(1)}, f32[8,10,4096]{2,1,0:T(8,128)}, s32[]{:T(128)}) %tuple.42), condition=%wide.while_cond, body=%wide.while_body.sunk | while | flops 2 | bytes 427097 | solution.py:46
  69.8 0.1 constant_dynamic-slice_fusion.2
  69.9 0.5 slice.734
  70.4 1.5 bitcast_dynamic-update-slice_fusion.2
  71.9 0.1 constant_dynamic-slice_fusion.2
  71.9 0.5 slice.734
  72.5 1.5 bitcast_dynamic-update-slice_fusion.2
  73.9 0.1 constant_dynamic-slice_fusion.2
  74.0 0.5 slice.734
  74.5 1.5 bitcast_dynamic-update-slice_fusion.2
  76.0 0.1 constant_dynamic-slice_fusion.2
  76.1 0.5 slice.734
  76.6 1.5 bitcast_dynamic-update-slice_fusion.2
  78.1 0.1 constant_dynamic-slice_fusion.2
  78.2 0.5 slice.734
  78.7 1.5 bitcast_dynamic-update-slice_fusion.2
  80.2 0.1 constant_dynamic-slice_fusion.2
  80.3 0.5 slice.734
  80.8 1.5 bitcast_dynamic-update-slice_fusion.2
  82.3 0.1 constant_dynamic-slice_fusion.2
  82.4 0.5 slice.734
  82.9 1.5 bitcast_dynamic-update-slice_fusion.2
  84.4 0.1 constant_dynamic-slice_fusion.2
  84.4 0.5 slice.734
  84.9 1.5 bitcast_dynamic-update-slice_fusion.2
  86.4 2.4 copy.31
  88.8 0.0 copy-start.6
  88.8 3.9 %gather_fusion.1 = f32[55,8,4096]{2,1,0:T(8,128)} fusion(f32[8,10,4096]{2,0,1:T(8,128)S(1)} %copy.31, s32[1024]{0:T(1024)S(1)} %pad_clamp_fusion.1), kind=kCustom, calls=%fused_computation.3 | custom fusion | bytes 14418140 | tf_op jit(solution)/shard_map/while/body/eval_jaxpr/gather | solution.py:52
  92.7 4.0 %gather_fusion.2 = f32[55,8,4096]{2,1,0:T(8,128)} fusion(f32[8,10,4096]{2,0,1:T(8,128)S(1)} %copy.31, s32[1024]{0:T(1024)S(1)} %pad_clamp_fusion), kind=kCustom, calls=%fused_computation.4 | custom fusion | bytes 14418140 | tf_op jit(solution)/shard_map/while/body/eval_jaxpr/gather | solution.py:52
  96.7 0.1 eq.109
  96.8 0.1 eq.105
  96.8 1.7 convolution_bitcast_fusion.2
  98.6 1.3 fusion.98
  99.8 5.4 %all_gather.7 = bf16[16,4096]{1,0:T(8,128)(2,1)S(1)} all-gather(bf16[16,1024]{1,0:T(8,128)(2,1)S(1)} %get-tuple-element.58), channel_id=1, replica_groups=mesh['tgt'=8,'band'=4] {'band'}, dimensions={1}, use_global_device_ids=true | all-gather | bytes 163840 | tf_op jit(solution)/shard_map/all_gather | solution.py:149
  105.2 5.4 %all_gather.6 = bf16[16,4096]{1,0:T(8,128)(2,1)S(1)} all-gather(bf16[16,1024]{1,0:T(8,128)(2,1)S(1)} %get-tuple-element.60), channel_id=1, replica_groups=mesh['tgt'=8,'band'=4] {'band'}, dimensions={1}, use_global_device_ids=true | all-gather | bytes 163840 | tf_op jit(solution)/shard_map/all_gather | solution.py:152
  110.6 2.6 convolution_bitcast_fusion
  113.3 7.2 %fusion.4 = f32[55,8,16]{2,1,0:T(8,128)S(1)} fusion(f32[55,8,4096]{2,1,0:T(8,128)} %gather_fusion.1, f32[55,8,4096]{2,1,0:T(8,128)} %gather_fusion.2, bf16[16,4096]{1,0:T(8,128)(2,1)S(1)} %all_gather.7), kind=kOutput, calls=%fused_computation.15 | convolution fusion | flops 347832320 | bytes 14577152 | tf_op jit(solution)/shard_map/while/body/eval_jaxpr/ti,zpi->ztp/dot_general | solution.py:53
  120.5 0.8 add_bitcast_fusion
  121.3 0.1 convert_multiply_fusion.1
  121.4 73.0 %all-to-all-done.2 = bf16[8,32,11,1024]{3,1,2,0:T(8,128)(2,1)} async-done(((bf16[8,32,11,1024]{3,1,2,0:T(8,128)(2,1)}), bf16[8,32,11,1024]{3,1,2,0:T(8,128)(2,1)}, u32[]{:S(2)}, u32[]{:S(2)}) %all-to-all-start.2) | async-done | bytes 5767200 | tf_op jit(solution)/shard_map/all_to_all | solution.py:129
  194.5 8.8 %convert_multiply_fusion = f32[8,32,11,1024]{3,1,2,0:T(8,128)} fusion(bf16[8,32,11,1024]{3,1,2,0:T(8,128)(2,1)} %all-to-all-done.2, f32[8,32,1024]{2,1,0:T(8,128)S(1)} %convert_multiply_fusion.1), kind=kLoop, calls=%fused_computation.8 | loop fusion | flops 5767168 | bytes 18350080 | tf_op jit(solution)/shard_map/mul | solution.py:135
  203.3 17.5 %copy.29 = f32[8,32,11,1024]{3,2,1,0:T(8,128)} copy(f32[8,32,11,1024]{3,1,2,0:T(8,128)} %convert_multiply_fusion) | data formatting | bytes 23068672 | tf_op jit(solution)/shard_map/mul | solution.py:135
  220.7 21.9 %copy.33 = f32[32,8,11,1024]{3,1,2,0:T(8,128)} copy(f32[32,8,11,1024]{3,2,1,0:T(8,128)} %bitcast.396) | data formatting | bytes 23068672
  242.7 12.4 %copy.30 = f32[11264,256]{1,0:T(8,128)} copy(f32[11264,256]{0,1:T(8,128)} %bitcast.397) | data formatting | bytes 23068672 | tf_op jit(solution)/shard_map/dot_general | solution.py:142
  255.0 10.3 %fusion.3 = bf16[16,11,1024]{2,0,1:T(8,128)(2,1)} fusion(f32[11,1024,256]{2,1,0:T(8,128)} %bitcast.398, f32[16,1024]{1,0:T(8,128)S(1)} %get-tuple-element.73, s32[256]{0:T(256)S(1)} %eq.105, pred[256]{0:T(512)(128)(4,1)S(1)} %eq.109), kind=kOutput, calls=%fused_computation.14 | convolution fusion | flops 554016768 | bytes 11961600 | tf_op jit(solution)/shard_map/dot_general | solution.py:142
  (29 shorter events, 0.1 us)
Async XLA Ops:
  0.6 36.4 %copy-start = (bf16[128,11,1024]{2,0,1:T(8,128)(2,1)S(1)}, bf16[128,11,1024]{2,0,1:T(8,128)(2,1)}, u32[]{:S(2)}) copy-start(bf16[128,11,1024]{2,0,1:T(8,128)(2,1)} %param.15) | copy-start | bytes 8650756
  0.6 6.3 %copy-start.2 = (bf16[128,1024]{1,0:T(8,128)(2,1)S(1)}, bf16[128,1024]{1,0:T(8,128)(2,1)}, u32[]{:S(2)}) copy-start(bf16[128,1024]{1,0:T(8,128)(2,1)} %param.13) | copy-start | bytes 786436
  32.6 30.2 %all-to-all-start.1 = ((bf16[8,32,1024]{2,1,0:T(8,128)(2,1)}), bf16[8,32,1024]{2,1,0:T(8,128)(2,1)}, u32[]{:S(2)}, u32[]{:S(2)}) async-start(bf16[8,32,1024]{2,1,0:T(8,128)(2,1)} %bitcast.400), calls=%async_computation.1 | async-start | bytes 1048576 | tf_op jit(solution)/shard_map/all_to_all | solution.py:127
  62.8 6.1 %copy-start.4 = (s32[1024]{0:T(1024)S(1)}, s32[1024]{0:T(1024)}, u32[]{:S(2)}) copy-start(s32[1024]{0:T(1024)} %param.16) | copy-start | bytes 12292
  62.8 6.4 %copy-start.5 = (s32[1024]{0:T(1024)S(1)}, s32[1024]{0:T(1024)}, u32[]{:S(2)}) copy-start(s32[1024]{0:T(1024)} %param.17) | copy-start | bytes 12292
  62.8 6.9 %copy-start.8 = (s32[32]{0:T(128)S(1)}, s32[32]{0:T(128)}, u32[]{:S(2)}) copy-start(s32[32]{0:T(128)} %param.19) | copy-start | bytes 388
  62.8 7.0 %copy-start.3 = (f32[10,4608]{1,0:T(8,128)S(1)}, f32[10,4608]{1,0:T(8,128)}, u32[]{:S(2)}) copy-start(f32[10,4608]{1,0:T(8,128)} %param.18) | copy-start | bytes 552964
  62.8 26.0 %copy-start.7 = (s32[55]{0:T(128)S(1)}, s32[55]{0:T(128)}, u32[]{:S(2)}) copy-start(s32[55]{0:T(128)} %constant.141) | copy-start | bytes 664
  62.8 131.6 %all-to-all-start.2 = ((bf16[8,32,11,1024]{3,1,2,0:T(8,128)(2,1)}), bf16[8,32,11,1024]{3,1,2,0:T(8,128)(2,1)}, u32[]{:S(2)}, u32[]{:S(2)}) async-start(bf16[8,32,11,1024]{3,1,2,0:T(8,128)(2,1)} %copy_select_fusion), calls=%async_computation.2 | async-start | bytes 11534336 | tf_op jit(solution)/shard_map/all_to_all | solution.py:129
  88.8 3.9 %copy-start.6 = (s32[55]{0:T(128)S(1)}, s32[55]{0:T(128)}, u32[]{:S(2)}) copy-start(s32[55]{0:T(128)} %constant.142) | copy-start | bytes 664
  242.7 22.7 %copy-start.1 = (bf16[128,11,1024]{2,0,1:T(8,128)(2,1)S(1)}, bf16[128,11,1024]{2,0,1:T(8,128)(2,1)}, u32[]{:S(2)}) copy-start(bf16[128,11,1024]{2,0,1:T(8,128)(2,1)} %param.15) | copy-start | bytes 8650756
where the time goes:
time: 269 us; the launch traced here: 266 us
  local copies, waits for them, and re-layouts  105 us (39%)
  waiting for transfers between devices  73 us (27%)
  blocking collectives  32.4 us (12%)
  matrix products  23.1 us (9%)
  other arithmetic  20.3 us (8%)
  starting transfers between devices  10.4 us (4%)
    all_to_all x1, waiting for transfers between devices, shards(): lax.all_to_all(outgoing[2], 'tgt', split_axis=0, concat_axis=0, tiled=True)  73 us
    gather x3, local copies, waits for them, and re-layouts, packed(): gathered = jnp.take(values, source_row, axis=0, mode='fill', fill_value=0)  25.5 us
    unnamed x19, local copies, waits for them, and re-layouts  22 us
    all_to_all x1, blocking collectives, shards(): lax.all_to_all(outgoing[1], 'tgt', split_axis=0, concat_axis=0, tiled=True)  21.6 us
    mul x1, local copies, waits for them, and re-layouts, shards(): weight[:, :, None, :] * got_res.astype(jnp.float32)  17.5 us
    gather x24, local copies, waits for them, and re-layouts  16.6 us
    dot_general x1, local copies, waits for them, and re-layouts, shards(): jnp.dot(member, res_terms, precision=lax.Precision.HIGHEST)  12.4 us
    dot_general x1, matrix products, shards(): jnp.dot(member, res_terms, precision=lax.Precision.HIGHEST)  10.3 us
  transfers between devices with their start and end apart: 2, of which 1 were waited for; matrix products, arithmetic and copies ran while one was open for 25% of the time, Pallas kernels for 0%

commit v1 on v0

--- a/solution.py
+++ b/solution.py
@@ -1,12 +1,21 @@
+import functools
+
 import jax
 import jax.numpy as jnp
 import numpy as np
 from jax import lax
+from jax.experimental import pallas as pl
+from jax.experimental.pallas import tpu as pltpu
 from jax.sharding import PartitionSpec as P
 
 TGT_DEV = 16
 NDIAG = 11
 Z_DEV = 8
+PIECE_LANES = 128
+FIT_LANES = 256
+AHEAD = 2
+VMEM_LIMIT = 48 * 1024 * 1024
+MESH = pl.DeviceIdType.MESH
 
 
 pair_first, pair_second = np.triu_indices(10)
@@ -160,8 +169,327 @@
     fit_gain = fit_from(matrix, right_side)
     return (coadd_flux, coadd_res, fit_gain)
 
+def as_bf16_parts(values, count):
+    parts = []
+    rest = values
+    for step in range(count):
+        part = rest.astype(jnp.bfloat16)
+        parts.append(part)
+        rest = rest - part.astype(jnp.float32)
+    return parts
+
+
+def exact_dot(left, right, dims, count):
+    total = None
+    for part in as_bf16_parts(left, count):
+        term = lax.dot_general(part, right, (dims, ((), ())), preferred_element_type=jnp.float32)
+        total = term if total is None else total + term
+    return total
+
+
+def partial_kernel(
+    target_s, valid_s, shift_s, target_v, valid_v, ivar, flux, res, basis,
+    wf_out, res_out, win_out, weight, totals, packed, rest16,
+):
+    owners = target_v.shape[0]
+    rows = ivar.shape[0]
+    pieces = res_out.shape[0]
+    lanes = res_out.shape[-1]
+    waves = win_out.shape[2]
+    device = lax.axis_index("tgt")
+    first_row = device * rows
+    ivar_all = ivar[...]
+    weight[...] = ivar_all.astype(jnp.float32)
+    totals[...] = jnp.zeros_like(totals)
+
+    def add_row(r, carry):
+        target = target_s[first_row + r]
+        flag = valid_s[first_row + r].astype(jnp.float32)
+        row = weight[pl.ds(r, 1), :] * flag
+        totals[target] = totals[target] + row * res[r].astype(jnp.float32)
+        return carry
+
+    lax.fori_loop(0, rows, add_row, 0, unroll=4)
+
+    own_target = target_v[pl.ds(device, 1), :]
+    own_valid = valid_v[pl.ds(device, 1), :]
+    ids = lax.broadcasted_iota(jnp.int32, (owners * TGT_DEV, rows), 0)
+    member = jnp.where(ids == own_target, own_valid, 0).astype(jnp.float32).astype(jnp.bfloat16)
+    dims = ((1,), (0,))
+    weight_part = lax.dot_general(
+        member, ivar_all, (dims, ((), ())), preferred_element_type=jnp.float32
+    )
+    product = weight[...] * flux[...].astype(jnp.float32)
+    flux_part = None
+    for part in as_bf16_parts(product, 2):
+        term = lax.dot_general(member, part, (dims, ((), ())), preferred_element_type=jnp.float32)
+        flux_part = term if flux_part is None else flux_part + term
+    for o in range(owners):
+        span = slice(o * TGT_DEV, (o + 1) * TGT_DEV)
+        wf_out[o % 2, o // 2, 0:TGT_DEV, :] = weight_part[span].astype(jnp.bfloat16)
+        wf_out[o % 2, o // 2, TGT_DEV:, :] = flux_part[span].astype(jnp.bfloat16)
+
+    def pack_owner(o, carry):
+        for t in range(TGT_DEV):
+            packed[t * NDIAG : (t + 1) * NDIAG, :] = totals[o * TGT_DEV + t]
+        for p in range(pieces):
+            res_out[p, o % 2, o // 2] = packed[:, p * lanes : (p + 1) * lanes].astype(jnp.bfloat16)
+        return carry
+
+    lax.fori_loop(0, owners, pack_owner, 0)
+
+    basis_count = basis.shape[0]
+    rest16[...] = jnp.zeros_like(rest16)
+    rest16[0:basis_count, :] = basis[...]
+    band = lax.axis_index("band")
+    for z in range(Z_DEV):
+        shift = shift_s[band * Z_DEV + z]
+        start = pl.multiple_of((shift // 128) * 128, 128)
+        wide = rest16[:, pl.ds(start, waves + 128)]
+        moved = pltpu.roll(wide, (waves + 128) - shift % 128, 1)
+        for b in range(basis_count):
+            win_out[b, z : z + 1, :] = moved[b : b + 1, 0:waves]
+
+
+def exchange_kernel(
+    wf, res, win, flux_out, res_out, gain_out,
+    wf_x, res_x, wf_to, res_to, wf_z, res_z, wf_own, res_own, band_own, band_in,
+    normal, right, final, inverse,
+    x_send, x_recv, z_send, z_recv, b_send, b_recv,
+):
+    pieces = res.shape[0]
+    high_count = res.shape[2]
+    lanes = res.shape[-1]
+    bands = lax.axis_size("band")
+    owners = lax.axis_size("tgt")
+    wave_dev = wf.shape[-1]
+    device = lax.axis_index("tgt")
+    band = lax.axis_index("band")
+    high = device // 2
+    low = device % 2
+    partner = high * 2 + (1 - low)
+
+    def peer(d):
+        return lax.rem(high + d, high_count) * 2 + low
+
+    def band_peer(d):
+        return lax.rem(band + d, bands)
+
+    barrier = pltpu.get_barrier_semaphore()
+    near = [(partner, band)]
+    near += [(peer(d), band) for d in range(1, high_count)]
+    near += [(device, band_peer(d)) for d in range(1, bands)]
+    for place in near:
+        pl.semaphore_signal(barrier, inc=1, device_id=place, device_id_type=MESH)
+    pl.semaphore_wait(barrier, len(near))
+
+    def copy(source, target, send, recv, place):
+        return pltpu.make_async_remote_copy(
+            src_ref=source, dst_ref=target, send_sem=send, recv_sem=recv,
+            device_id=place, device_id_type=MESH,
+        )
+
+    x_copies = [copy(wf.at[1 - low], wf_x, x_send.at[0], x_recv.at[0], (partner, band))]
+    for p in range(pieces):
+        x_copies.append(
+            copy(res.at[p, 1 - low], res_x.at[p], x_send.at[p + 1], x_recv.at[p + 1], (partner, band))
+        )
+    z_copies = []
+    for p in range(pieces + 1):
+        row = []
+        for d in range(1, high_count):
+            source = wf_to.at[d - 1] if p == 0 else res_to.at[p - 1, d - 1]
+            target = wf_z.at[d - 1] if p == 0 else res_z.at[p - 1, d - 1]
+            row.append(
+                copy(source, target, z_send.at[p, d - 1], z_recv.at[p, d - 1], (peer(d), band))
+            )
+        z_copies.append(row)
+    b_copies = [
+        copy(band_own, band_in.at[d - 1], b_send.at[d - 1], b_recv.at[d - 1], (device, band_peer(d)))
+        for d in range(1, bands)
+    ]
+
+    def relay(p):
+        x_copies[p].wait_recv()
+        if p + AHEAD < len(x_copies):
+            x_copies[p + AHEAD].start()
+        for d in range(1, high_count):
+            h = lax.rem(high + d, high_count)
+            if p == 0:
+                total = wf[low, h].astype(jnp.float32) + wf_x[h].astype(jnp.float32)
+                wf_to[d - 1] = total.astype(jnp.bfloat16)
+            else:
+                total = res[p - 1, low, h].astype(jnp.float32) + res_x[p - 1, h].astype(jnp.float32)
+                res_to[p - 1, d - 1] = total.astype(jnp.bfloat16)
+            z_copies[p][d - 1].start()
+        if p == 0:
+            wf_own[...] = wf[low, high].astype(jnp.float32) + wf_x[high].astype(jnp.float32)
+        else:
+            res_own[p - 1] = (
+                res[p - 1, low, high].astype(jnp.float32) + res_x[p - 1, high].astype(jnp.float32)
+            )
+
+    def finish_sums():
+        total = wf_own[...]
+        for d in range(1, high_count):
+            z_copies[0][d - 1].wait_recv()
+            total = total + wf_z[d - 1].astype(jnp.float32)
+        band_own[...] = total.astype(jnp.bfloat16)
+        for step in b_copies:
+            step.start()
+        weight_sum = total[0:TGT_DEV]
+        flux_out[...] = total[TGT_DEV:] / weight_sum
+        inverse[...] = 1.0 / weight_sum
+
+    def fit_block(d):
+        if d == 0:
+            source, place = band_own, band
+        else:
+            b_copies[d - 1].wait_recv()
+            source, place = band_in.at[d - 1], lax.rem(band + (bands - d), bands)
+        dims = ((1,), (1,))
+        for step in range(wave_dev // FIT_LANES):
+            span = slice(step * FIT_LANES, (step + 1) * FIT_LANES)
+            at = pl.multiple_of(place * wave_dev + step * FIT_LANES, FIT_LANES)
+            waves = [win[b, :, pl.ds(at, FIT_LANES)] for b in range(win.shape[0])]
+            pairs = [waves[int(b)] * waves[int(c)] for b, c in zip(pair_first, pair_second)]
+            pairs.append(pairs[0])
+            matrix = exact_dot(jnp.concatenate(pairs, axis=0), source[0:TGT_DEV, span], dims, 3)
+            sides = exact_dot(jnp.concatenate(waves, axis=0), source[TGT_DEV:, span], dims, 3)
+            if d == 0 and step == 0:
+                normal[...] = matrix
+                right[...] = sides
+            else:
+                normal[...] += matrix
+                right[...] += sides
+
+    def solve():
+        matrix = [normal[Z_DEV * p : Z_DEV * (p + 1), :] for p in range(len(pair_first))]
+        sides = [right[Z_DEV * b : Z_DEV * (b + 1), :] for b in range(win.shape[0])]
+        gain_out[...] = solve_normal(matrix, jnp.stack(sides))
+
+    def finish_piece(p):
+        total = res_own[p]
+        for d in range(1, high_count):
+            z_copies[p + 1][d - 1].wait_recv()
+            total = total + res_z[p, d - 1].astype(jnp.float32)
+        final[...] = total
+        span = slice(p * lanes, (p + 1) * lanes)
+        for t in range(TGT_DEV):
+            one = final[t * NDIAG : (t + 1) * NDIAG, :] * inverse[t : t + 1, span]
+            res_out[t, :, span] = one.astype(jnp.bfloat16)
+
+    for p in range(min(AHEAD, len(x_copies))):
+        x_copies[p].start()
+    jobs = [finish_sums] + [functools.partial(fit_block, d) for d in range(bands)] + [solve]
+    relay(0)
+    finished = 0
+    for p in range(1, pieces + 1):
+        relay(p)
+        if jobs:
+            jobs.pop(0)()
+        if p >= 4:
+            finish_piece(finished)
+            finished += 1
+    while jobs:
+        jobs.pop(0)()
+    while finished < pieces:
+        finish_piece(finished)
+        finished += 1
+    for step in x_copies + b_copies + [step for row in z_copies for step in row]:
+        step.wait_send()
+
+
+def dense_shards(
+    exposure_flux, exposure_ivar, exposure_res, target_of_row, valid_of_row, rest_basis, redshift_shift
+):
+    owners = lax.axis_size("tgt")
+    bands = lax.axis_size("band")
+    rows, wave_dev = exposure_flux.shape
+    waves = wave_dev * bands
+    basis_count = rest_basis.shape[0]
+    high_count = owners // 2
+    pieces = wave_dev // PIECE_LANES
+    packed_rows = TGT_DEV * NDIAG
+    pair_rows = Z_DEV * (len(pair_first) + 1)
+    vmem = pl.BlockSpec(memory_space=pltpu.VMEM)
+    smem = pl.BlockSpec(memory_space=pltpu.SMEM)
+    half, full = jnp.bfloat16, jnp.float32
+    wf, res, win = pl.pallas_call(
+        partial_kernel,
+        out_shape=(
+            jax.ShapeDtypeStruct((2, high_count, 2 * TGT_DEV, wave_dev), half),
+            jax.ShapeDtypeStruct((pieces, 2, high_count, packed_rows, PIECE_LANES), half),
+            jax.ShapeDtypeStruct((basis_count, Z_DEV, waves), full),
+        ),
+        in_specs=[smem] * 3 + [vmem] * 6,
+        out_specs=(vmem, vmem, vmem),
+        scratch_shapes=[
+            pltpu.VMEM((rows, wave_dev), full),
+            pltpu.VMEM((owners * TGT_DEV, NDIAG, wave_dev), full),
+            pltpu.VMEM((packed_rows, wave_dev), full),
+            pltpu.VMEM((16, rest_basis.shape[1]), full),
+        ],
+        compiler_params=pltpu.CompilerParams(vmem_limit_bytes=VMEM_LIMIT),
+        name="partial_sums",
+    )(
+        target_of_row, valid_of_row, redshift_shift,
+        target_of_row.reshape(owners, rows), valid_of_row.reshape(owners, rows),
+        exposure_ivar, exposure_flux, exposure_res, rest_basis,
+    )
+    peers = high_count - 1
+    block = (packed_rows, PIECE_LANES)
+    sums = (2 * TGT_DEV, wave_dev)
+    dma = pltpu.SemaphoreType.DMA
+    coadd_flux, coadd_res, gain = pl.pallas_call(
+        exchange_kernel,
+        out_shape=(
+            jax.ShapeDtypeStruct((TGT_DEV, wave_dev), full),
+            jax.ShapeDtypeStruct((TGT_DEV, NDIAG, wave_dev), half),
+            jax.ShapeDtypeStruct((Z_DEV, TGT_DEV), full),
+        ),
+        in_specs=[vmem] * 3,
+        out_specs=(vmem, vmem, vmem),
+        scratch_shapes=[
+            pltpu.VMEM((high_count,) + sums, half),
+            pltpu.VMEM((pieces, high_count) + block, half),
+            pltpu.VMEM((peers,) + sums, half),
+            pltpu.VMEM((pieces, peers) + block, half),
+            pltpu.VMEM((peers,) + sums, half),
+            pltpu.VMEM((pieces, peers) + block, half),
+            pltpu.VMEM(sums, full),
+            pltpu.VMEM((pieces,) + block, full),
+            pltpu.VMEM(sums, half),
+            pltpu.VMEM((bands - 1,) + sums, half),
+            pltpu.VMEM((pair_rows, TGT_DEV), full),
+            pltpu.VMEM((Z_DEV * basis_count, TGT_DEV), full),
+            pltpu.VMEM(block, full),
+            pltpu.VMEM((TGT_DEV, wave_dev), full),
+            dma((pieces + 1,)),
+            dma((pieces + 1,)),
+            dma((pieces + 1, peers)),
+            dma((pieces + 1, peers)),
+            dma((bands - 1,)),
+            dma((bands - 1,)),
+        ],
+        compiler_params=pltpu.CompilerParams(
+            vmem_limit_bytes=VMEM_LIMIT, collective_id=0, has_side_effects=True
+        ),
+        name="exchange_and_fit",
+    )(wf, res, win)
+    return (coadd_flux, coadd_res, gain.T)
+
 
 def solution(mesh):
     in_specs = (P("tgt", "band"), P("tgt", "band"), P("tgt", None, "band"), P(), P(), P(), P())
     out_specs = (P("tgt", "band"), P("tgt", None, "band"), P("tgt", "band"))
-    return jax.shard_map(shards, mesh=mesh, in_specs=in_specs, out_specs=out_specs, check_vma=False)
+    owners = mesh.shape["tgt"]
+
+    def whole(*args):
+        rows = args[0].shape[0] // owners
+        body = dense_shards if owners * TGT_DEV <= 2 * rows and owners % 2 == 0 else shards
+        return jax.shard_map(
+            body, mesh=mesh, in_specs=in_specs, out_specs=out_specs, check_vma=False
+        )(*args)
+
+    return whole

time: 269 us -> 66.6 us (0.25); the launches traced: 266 us -> 66.4 us
  local copies, waits for them, and re-layouts: 105 us -> 7.75 us
  waiting for transfers between devices: 73 us -> 0 us
  Pallas kernels: 0 us -> 57.9 us
  blocking collectives: 32.4 us -> 0 us
  matrix products: 23.1 us -> 0 us
  other arithmetic: 20.3 us -> 0 us
  starting transfers between devices: 10.4 us -> 0 us
    all_to_all x2 -> x0, waiting for transfers between devices: 73 us -> none  [the longest x1 73 us: shards(): lax.all_to_all(outgoing[2], 'tgt', split_axis=0, concat_axis=0, tiled=True)]
    pallas_call x0 -> x2, Pallas kernels: none -> 57.9 us  [the longest x1 51.1 us: dense_shards(): pl.pallas_call(exchange_kernel, out_shape=(jax.ShapeDtypeStruct((TGT_DEV,...]
    gather x30 -> x0, local copies, waits for them, and re-layouts: 52.3 us -> none  [the longest x3 25.5 us: packed(): gathered = jnp.take(values, source_row, axis=0, mode='fill', fill_value=0)]
    dot_general x5 -> x0, matrix products: 23.1 us -> none  [the longest x1 10.3 us: shards(): jnp.dot(member, res_terms, precision=lax.Precision.HIGHEST)]
    all_to_all x1 -> x0, blocking collectives: 21.6 us -> none  [shards(): lax.all_to_all(outgoing[1], 'tgt', split_axis=0, concat_axis=0, tiled=True)]
    mul x1 -> x0, local copies, waits for them, and re-layouts: 17.5 us -> none  [shards(): weight[:, :, None, :] * got_res.astype(jnp.float32)]
    unnamed x19 -> x16, local copies, waits for them, and re-layouts: 22 us -> 7.75 us
    dot_general x1 -> x0, local copies, waits for them, and re-layouts: 12.4 us -> none  [shards(): jnp.dot(member, res_terms, precision=lax.Precision.HIGHEST)]
  transfers between devices with their start and end apart: 2 -> 0, of which waited for: 1 -> 0; matrix products, arithmetic and copies ran while one was open for 25% -> 0% of each run, Pallas kernels for 0% -> 0%
where the time goes in v1:
time: 66.6 us; the launch traced here: 66.4 us
  Pallas kernels  57.9 us (87%)
  local copies, waits for them, and re-layouts  7.75 us (12%)
  between operations  0.73 us (1%)
    pallas_call x1, Pallas kernels, dense_shards(): pl.pallas_call(exchange_kernel, out_shape=(jax.ShapeDtypeStruct((TGT_DEV,...  51.1 us
    unnamed x16, local copies, waits for them, and re-layouts  7.75 us
    pallas_call x1, Pallas kernels, dense_shards(): pl.pallas_call(partial_kernel, out_shape=(jax.ShapeDtypeStruct((2, high_c...  6.81 us

profile of v1, /device:TPU:0, one launch (start us, length us, event | category | flops | bytes accessed | tf_op | source)
XLA Modules:
  0.0 66.4 jit_solution(14579031784539249309)
XLA Ops:
  0.6 0.0 copy-start
  0.6 0.0 copy-start.1
  0.7 0.0 copy-start.2
  0.7 0.0 copy-start.3
  0.7 0.0 copy-start.4
  0.7 0.0 copy-start.5
  0.7 5.6 %copy.10.res = bf16[128,11,1024]{2,1,0:T(8,128)(2,1)} copy(bf16[128,11,1024]{2,0,1:T(8,128)(2,1)} %param.9) | data formatting | bytes 5767168 | tf_op args[2]
  6.2 0.0 copy-done
  6.2 0.0 copy-done.1
  6.2 0.0 copy-done.2
  6.3 0.0 copy-done.3
  6.3 0.0 copy-done.4
  6.3 0.0 copy-done.5
  6.3 6.8 %partial_sums.1 = (bf16[2,4,32,1024]{3,2,1,0:T(8,128)(2,1)S(1)}, bf16[8,2,4,176,128]{4,3,2,1,0:T(8,128)(2,1)S(1)}, f32[10,8,4096]{2,1,0:T(8,128)S(1)}) custom-call(s32[1024]{0:T(1024)S(1)} %copy-done.3, s32[1024]{0:T(1024)S(1)} %copy-done.4, s32[32]{0:T(128)S(1)} %copy-done.5, s32[8,128]{1,0:T(8,128)S(1)} %bitcast.3, s32[8,128]{1,0:T(8,128)S(1)} %bitcast.4, ...), custom_call_target="tpu_custom_call" | custom-call | tf_op jit(solution)/shard_map/partial_sums/pallas_call | solution.py:418
  13.1 51.1 %exchange_and_fit.1 = (f32[16,1024]{1,0:T(8,128)S(1)}, bf16[16,11,1024]{2,1,0:T(8,128)(2,1)S(1)}, f32[8,16]{1,0:T(8,128)S(1)}) custom-call(bf16[2,4,32,1024]{3,2,1,0:T(8,128)(2,1)S(1)} %get-tuple-element.9.wf, bf16[8,2,4,176,128]{4,3,2,1,0:T(8,128)(2,1)S(1)} %get-tuple-element.10.res, f32[10,8,4096]{2,1,0:T(8,128)S(1)} %get-tuple-element.11.win), custom_call_target="tpu_custom_call" | custom-call | tf_op jit(solution)/shard_map/exchange_and_fit/pallas_call | solution.py:444
  64.2 1.0 %copy.11 = bf16[16,11,1024]{2,0,1:T(8,128)(2,1)} copy(bf16[16,11,1024]{2,1,0:T(8,128)(2,1)S(1)} %get-tuple-element.16) | data formatting | bytes 720896
  65.2 0.6 copy.14
  65.8 0.6 copy.15
Async XLA Ops:
  0.6 5.6 %copy-start = (f32[10,4608]{1,0:T(8,128)S(1)}, f32[10,4608]{1,0:T(8,128)}, u32[]{:S(2)}) copy-start(f32[10,4608]{1,0:T(8,128)} %basis.1) | copy-start | bytes 552964
  0.6 5.6 %copy-start.1 = (bf16[128,1024]{1,0:T(8,128)(2,1)S(1)}, bf16[128,1024]{1,0:T(8,128)(2,1)}, u32[]{:S(2)}) copy-start(bf16[128,1024]{1,0:T(8,128)(2,1)} %ivar.1) | copy-start | bytes 786436
  0.7 5.6 %copy-start.2 = (bf16[128,1024]{1,0:T(8,128)(2,1)S(1)}, bf16[128,1024]{1,0:T(8,128)(2,1)}, u32[]{:S(2)}) copy-start(bf16[128,1024]{1,0:T(8,128)(2,1)} %flux.1) | copy-start | bytes 786436
  0.7 5.6 %copy-start.3 = (s32[1024]{0:T(1024)S(1)}, s32[1024]{0:T(1024)}, u32[]{:S(2)}) copy-start(s32[1024]{0:T(1024)} %target_s.1) | copy-start | bytes 12292
  0.7 5.6 %copy-start.4 = (s32[1024]{0:T(1024)S(1)}, s32[1024]{0:T(1024)}, u32[]{:S(2)}) copy-start(s32[1024]{0:T(1024)} %valid_s.1) | copy-start | bytes 12292
  0.7 5.6 %copy-start.5 = (s32[32]{0:T(128)S(1)}, s32[32]{0:T(128)}, u32[]{:S(2)}) copy-start(s32[32]{0:T(128)} %shift_s.1) | copy-start | bytes 388

commit v2 on v0

--- a/solution.py
+++ b/solution.py
@@ -1,12 +1,20 @@
+import functools
+
 import jax
 import jax.numpy as jnp
 import numpy as np
 from jax import lax
+from jax.experimental import pallas as pl
+from jax.experimental.pallas import tpu as pltpu
 from jax.sharding import PartitionSpec as P
 
 TGT_DEV = 16
 NDIAG = 11
 Z_DEV = 8
+FIT_LANES = 256
+AHEAD = 3
+VMEM_LIMIT = 60 * 1024 * 1024
+MESH = pl.DeviceIdType.MESH
 
 
 pair_first, pair_second = np.triu_indices(10)
@@ -160,8 +168,326 @@
     fit_gain = fit_from(matrix, right_side)
     return (coadd_flux, coadd_res, fit_gain)
 
+def as_bf16_parts(values, count):
+    parts = []
+    rest = values
+    for step in range(count):
+        part = rest.astype(jnp.bfloat16)
+        parts.append(part)
+        rest = rest - part.astype(jnp.float32)
+    return parts
+
+
+def exact_dot(left, right, dims, count):
+    total = None
+    for part in as_bf16_parts(left, count):
+        term = lax.dot_general(part, right, (dims, ((), ())), preferred_element_type=jnp.float32)
+        total = term if total is None else total + term
+    return total
+
+
+def fused_kernel(
+    shift_s, target_v, valid_v, basis, ivar_any, flux_any, res_any,
+    flux_out, res_out, gain_out,
+    ivar, flux, res, weight, doubled, win,
+    sums_x, sums_in, sums_to, sums_z, sums_own,
+    res_x, res_in, res_to, res_z, res_own,
+    band_own, band_in, normal, right, inverse,
+    l_sem, x_send, x_recv, z_send, z_recv, b_send, b_recv,
+):
+    owners, rows = target_v.shape
+    channels, wave_dev = res.shape[0], res.shape[-1]
+    bands = lax.axis_size("band")
+    high_count = owners // 2
+    waves = win.shape[2]
+    basis_count = basis.shape[0]
+    device = lax.axis_index("tgt")
+    band = lax.axis_index("band")
+    high = device // 2
+    low = device % 2
+    partner = high * 2 + (1 - low)
+
+    def peer(d):
+        return lax.rem(high + d, high_count) * 2 + low
+
+    def band_peer(d):
+        return lax.rem(band + d, bands)
+
+    loads = [
+        pltpu.make_async_copy(ivar_any, ivar, l_sem.at[0]),
+        pltpu.make_async_copy(flux_any, flux, l_sem.at[1]),
+    ]
+    for k in range(channels):
+        loads.append(pltpu.make_async_copy(res_any.at[k], res.at[k], l_sem.at[k + 2]))
+    for step in loads:
+        step.start()
+
+    barrier = pltpu.get_barrier_semaphore()
+    near = [(partner, band)]
+    near += [(peer(d), band) for d in range(1, high_count)]
+    near += [(device, band_peer(d)) for d in range(1, bands)]
+    for place in near:
+        pl.semaphore_signal(barrier, inc=1, device_id=place, device_id_type=MESH)
+
+    def copy(source, target, send, recv, place):
+        return pltpu.make_async_remote_copy(
+            src_ref=source, dst_ref=target, send_sem=send, recv_sem=recv,
+            device_id=place, device_id_type=MESH,
+        )
+
+    x_copies = [copy(sums_x, sums_in, x_send.at[0], x_recv.at[0], (partner, band))]
+    for k in range(channels):
+        x_copies.append(
+            copy(res_x.at[k], res_in.at[k], x_send.at[k + 1], x_recv.at[k + 1], (partner, band))
+        )
+    z_copies = []
+    for p in range(channels + 1):
+        row = []
+        for d in range(1, high_count):
+            source = sums_to.at[d - 1] if p == 0 else res_to.at[p - 1, d - 1]
+            target = sums_z.at[d - 1] if p == 0 else res_z.at[p - 1, d - 1]
+            row.append(
+                copy(source, target, z_send.at[p, d - 1], z_recv.at[p, d - 1], (peer(d), band))
+            )
+        z_copies.append(row)
+    b_copies = [
+        copy(band_own, band_in.at[d - 1], b_send.at[d - 1], b_recv.at[d - 1], (device, band_peer(d)))
+        for d in range(1, bands)
+    ]
+
+    count = owners * TGT_DEV
+    half = count // 2
+    ids = lax.broadcasted_iota(jnp.int32, (count, rows), 0)
+    own_half = (ids >= half).astype(jnp.int32)
+    distance = (ids - own_half * half) // TGT_DEV
+    row_low = own_half * low + (1 - own_half) * (1 - low)
+    row_target = (lax.rem(distance + high, high_count) * 2 + row_low) * TGT_DEV + ids % TGT_DEV
+    own_target = target_v[pl.ds(device, 1), :]
+    own_valid = valid_v[pl.ds(device, 1), :]
+    member = jnp.where(row_target == own_target, own_valid, 0).astype(jnp.float32)
+    member = member.astype(jnp.bfloat16)
+    doubled[...] = jnp.concatenate([member, member], axis=1)
+    dims = (((1,), (0,)), ((), ()))
+
+    def summed(values):
+        product = weight[...] * values.astype(jnp.float32)
+        parts = jnp.concatenate(as_bf16_parts(product, 2), axis=0)
+        return lax.dot_general(doubled[...], parts, dims, preferred_element_type=jnp.float32)
+
+    def prepare_sums():
+        loads[0].wait()
+        loads[1].wait()
+        weight[...] = ivar[...].astype(jnp.float32)
+        for place, part in (
+            (0, lax.dot_general(member, ivar[...], dims, preferred_element_type=jnp.float32)),
+            (TGT_DEV, summed(flux[...])),
+        ):
+            for d in range(high_count):
+                span = slice(d * TGT_DEV, (d + 1) * TGT_DEV)
+                other = slice(half + d * TGT_DEV, half + (d + 1) * TGT_DEV)
+                sums_x[d, place : place + TGT_DEV, :] = part[span].astype(jnp.bfloat16)
+                sums_own[d, place : place + TGT_DEV, :] = part[other]
+
+    def prepare(k):
+        loads[k + 2].wait()
+        part = summed(res[k])
+        for d in range(high_count):
+            span = slice(d * TGT_DEV, (d + 1) * TGT_DEV)
+            other = slice(half + d * TGT_DEV, half + (d + 1) * TGT_DEV)
+            res_x[k, d] = part[span].astype(jnp.bfloat16)
+            res_own[k, d] = part[other]
+
+    def relay(p):
+        x_copies[p].wait_recv()
+        if p + AHEAD <= channels:
+            prepare(p + AHEAD - 1)
+            x_copies[p + AHEAD].start()
+        for d in range(1, high_count):
+            if p == 0:
+                total = sums_own[d] + sums_in[d].astype(jnp.float32)
+                sums_to[d - 1] = total.astype(jnp.bfloat16)
+            else:
+                total = res_own[p - 1, d] + res_in[p - 1, d].astype(jnp.float32)
+                res_to[p - 1, d - 1] = total.astype(jnp.bfloat16)
+            z_copies[p][d - 1].start()
+
+    def finish_sums():
+        total = sums_own[0] + sums_in[0].astype(jnp.float32)
+        for d in range(1, high_count):
+            z_copies[0][d - 1].wait_recv()
+            total = total + sums_z[d - 1].astype(jnp.float32)
+        band_own[...] = total.astype(jnp.bfloat16)
+        for step in b_copies:
+            step.start()
+        weight_sum = total[0:TGT_DEV]
+        flux_out[...] = total[TGT_DEV:] / weight_sum
+        inverse[...] = 1.0 / weight_sum
+
+    def make_windows(first, last):
+        ids8 = lax.broadcasted_iota(jnp.int32, (Z_DEV, 128), 0)
+        shift = jnp.zeros((Z_DEV, 128), jnp.int32)
+        for z in range(Z_DEV):
+            shift = jnp.where(ids8 == z, shift_s[band * Z_DEV + z], shift)
+        spare = basis.shape[1] - waves
+
+        def one_basis(b, carry):
+            rows_of = jnp.broadcast_to(basis[pl.ds(b, 1), :], (Z_DEV, basis.shape[1]))
+            step = spare // 2
+            while step >= 1:
+                if step >= 128:
+                    width = rows_of.shape[1] - step
+                    moved, kept = rows_of[:, step:], rows_of[:, :width]
+                else:
+                    width = rows_of.shape[1]
+                    moved, kept = pltpu.roll(rows_of, width - step, 1), rows_of
+                wide = jnp.concatenate([shift] * (width // 128), axis=1)
+                rows_of = jnp.where((wide & step) != 0, moved, kept)
+                step //= 2
+            win[b] = rows_of[:, :waves]
+            return carry
+
+        lax.fori_loop(first, last, one_basis, 0)
+
+    def fit_block(d):
+        if d == 0:
+            source, place = band_own, band
+        else:
+            b_copies[d - 1].wait_recv()
+            source, place = band_in.at[d - 1], lax.rem(band + (bands - d), bands)
+        last = ((1,), (1,))
+        for step in range(wave_dev // FIT_LANES):
+            span = slice(step * FIT_LANES, (step + 1) * FIT_LANES)
+            at = pl.multiple_of(place * wave_dev + step * FIT_LANES, FIT_LANES)
+            bases = [win[b, :, pl.ds(at, FIT_LANES)] for b in range(basis_count)]
+            pairs = [bases[int(b)] * bases[int(c)] for b, c in zip(pair_first, pair_second)]
+            pairs.append(pairs[0])
+            matrix = exact_dot(jnp.concatenate(pairs, axis=0), source[0:TGT_DEV, span], last, 3)
+            sides = exact_dot(jnp.concatenate(bases, axis=0), source[TGT_DEV:, span], last, 3)
+            if d == 0 and step == 0:
+                normal[...] = matrix
+                right[...] = sides
+            else:
+                normal[...] += matrix
+                right[...] += sides
+
+    def solve():
+        matrix = [normal[Z_DEV * p : Z_DEV * (p + 1), :] for p in range(len(pair_first))]
+        sides = [right[Z_DEV * b : Z_DEV * (b + 1), :] for b in range(basis_count)]
+        gain_out[...] = solve_normal(matrix, jnp.stack(sides))
+
+    def finish(k):
+        total = res_own[k, 0] + res_in[k, 0].astype(jnp.float32)
+        for d in range(1, high_count):
+            z_copies[k + 1][d - 1].wait_recv()
+            total = total + res_z[k, d - 1].astype(jnp.float32)
+        res_out[k] = (total * inverse[...]).astype(jnp.bfloat16)
+
+    prepare_sums()
+    pl.semaphore_wait(barrier, len(near))
+    x_copies[0].start()
+    for p in range(1, AHEAD):
+        prepare(p - 1)
+        x_copies[p].start()
+    jobs = [functools.partial(make_windows, 0, basis_count // 2)]
+    jobs += [functools.partial(make_windows, basis_count // 2, basis_count), finish_sums]
+    jobs += [functools.partial(fit_block, d) for d in range(bands)] + [solve]
+    relay(0)
+    finished = 0
+    for p in range(1, channels + 1):
+        relay(p)
+        if jobs:
+            jobs.pop(0)()
+        if p >= 6:
+            finish(finished)
+            finished += 1
+    while jobs:
+        jobs.pop(0)()
+    while finished < channels:
+        finish(finished)
+        finished += 1
+    for step in x_copies + b_copies + [step for row in z_copies for step in row]:
+        step.wait_send()
+
+
+def dense_shards(
+    exposure_flux, exposure_ivar, exposure_res, target_of_row, valid_of_row, rest_basis, redshift_shift
+):
+    owners = lax.axis_size("tgt")
+    bands = lax.axis_size("band")
+    rows, wave_dev = exposure_flux.shape
+    waves = wave_dev * bands
+    basis_count = rest_basis.shape[0]
+    high_count = owners // 2
+    peers = high_count - 1
+    pair_rows = Z_DEV * (len(pair_first) + 1)
+    vmem = pl.BlockSpec(memory_space=pltpu.VMEM)
+    smem = pl.BlockSpec(memory_space=pltpu.SMEM)
+    hbm = pl.BlockSpec(memory_space=pl.ANY)
+    half, full = jnp.bfloat16, jnp.float32
+    block = (TGT_DEV, wave_dev)
+    sums = (2 * TGT_DEV, wave_dev)
+    dma = pltpu.SemaphoreType.DMA
+    coadd_flux, coadd_res, gain = pl.pallas_call(
+        fused_kernel,
+        out_shape=(
+            jax.ShapeDtypeStruct(block, full),
+            jax.ShapeDtypeStruct((NDIAG,) + block, half),
+            jax.ShapeDtypeStruct((Z_DEV, TGT_DEV), full),
+        ),
+        in_specs=[smem, vmem, vmem, vmem, hbm, hbm, hbm],
+        out_specs=(vmem, vmem, vmem),
+        scratch_shapes=[
+            pltpu.VMEM((rows, wave_dev), half),
+            pltpu.VMEM((rows, wave_dev), half),
+            pltpu.VMEM((NDIAG, rows, wave_dev), half),
+            pltpu.VMEM((rows, wave_dev), full),
+            pltpu.VMEM((owners * TGT_DEV, 2 * rows), half),
+            pltpu.VMEM((basis_count, Z_DEV, waves), full),
+            pltpu.VMEM((high_count,) + sums, half),
+            pltpu.VMEM((high_count,) + sums, half),
+            pltpu.VMEM((peers,) + sums, half),
+            pltpu.VMEM((peers,) + sums, half),
+            pltpu.VMEM((high_count,) + sums, full),
+            pltpu.VMEM((NDIAG, high_count) + block, half),
+            pltpu.VMEM((NDIAG, high_count) + block, half),
+            pltpu.VMEM((NDIAG, peers) + block, half),
+            pltpu.VMEM((NDIAG, peers) + block, half),
+            pltpu.VMEM((NDIAG, high_count) + block, full),
+            pltpu.VMEM(sums, half),
+            pltpu.VMEM((bands - 1,) + sums, half),
+            pltpu.VMEM((pair_rows, TGT_DEV), full),
+            pltpu.VMEM((Z_DEV * basis_count, TGT_DEV), full),
+            pltpu.VMEM(block, full),
+            dma((NDIAG + 2,)),
+            dma((NDIAG + 1,)),
+            dma((NDIAG + 1,)),
+            dma((NDIAG + 1, peers)),
+            dma((NDIAG + 1, peers)),
+            dma((bands - 1,)),
+            dma((bands - 1,)),
+        ],
+        compiler_params=pltpu.CompilerParams(
+            vmem_limit_bytes=VMEM_LIMIT, collective_id=0, has_side_effects=True
+        ),
+        name="coadd_and_fit",
+    )(
+        redshift_shift,
+        target_of_row.reshape(owners, rows), valid_of_row.reshape(owners, rows), rest_basis,
+        exposure_ivar, exposure_flux, jnp.transpose(exposure_res, (1, 0, 2)),
+    )
+    return (coadd_flux, jnp.transpose(coadd_res, (1, 0, 2)), gain.T)
+
 
 def solution(mesh):
     in_specs = (P("tgt", "band"), P("tgt", "band"), P("tgt", None, "band"), P(), P(), P(), P())
     out_specs = (P("tgt", "band"), P("tgt", None, "band"), P("tgt", "band"))
-    return jax.shard_map(shards, mesh=mesh, in_specs=in_specs, out_specs=out_specs, check_vma=False)
+    owners = mesh.shape["tgt"]
+
+    def whole(*args):
+        rows = args[0].shape[0] // owners
+        body = dense_shards if owners * TGT_DEV <= 2 * rows and owners % 2 == 0 else shards
+        return jax.shard_map(
+            body, mesh=mesh, in_specs=in_specs, out_specs=out_specs, check_vma=False
+        )(*args)
+
+    return whole

time: 269 us -> 58.9 us (0.22); the launches traced: 266 us -> 58.7 us
  local copies, waits for them, and re-layouts: 105 us -> 4.49 us
  waiting for transfers between devices: 73 us -> 0 us
  Pallas kernels: 0 us -> 53.6 us
  blocking collectives: 32.4 us -> 0 us
  matrix products: 23.1 us -> 0 us
  other arithmetic: 20.3 us -> 0 us
  starting transfers between devices: 10.4 us -> 0 us
    all_to_all x2 -> x0, waiting for transfers between devices: 73 us -> none  [the longest x1 73 us: shards(): lax.all_to_all(outgoing[2], 'tgt', split_axis=0, concat_axis=0, tiled=True)]
    pallas_call x0 -> x1, Pallas kernels: none -> 53.6 us  [dense_shards(): pl.pallas_call(fused_kernel, out_shape=(jax.ShapeDtypeStruct(block, full)...]
    gather x30 -> x0, local copies, waits for them, and re-layouts: 52.3 us -> none  [the longest x3 25.5 us: packed(): gathered = jnp.take(values, source_row, axis=0, mode='fill', fill_value=0)]
    dot_general x5 -> x0, matrix products: 23.1 us -> none  [the longest x1 10.3 us: shards(): jnp.dot(member, res_terms, precision=lax.Precision.HIGHEST)]
    all_to_all x1 -> x0, blocking collectives: 21.6 us -> none  [shards(): lax.all_to_all(outgoing[1], 'tgt', split_axis=0, concat_axis=0, tiled=True)]
    unnamed x19 -> x3, local copies, waits for them, and re-layouts: 22 us -> 4.49 us
    mul x1 -> x0, local copies, waits for them, and re-layouts: 17.5 us -> none  [shards(): weight[:, :, None, :] * got_res.astype(jnp.float32)]
    dot_general x1 -> x0, local copies, waits for them, and re-layouts: 12.4 us -> none  [shards(): jnp.dot(member, res_terms, precision=lax.Precision.HIGHEST)]
  transfers between devices with their start and end apart: 2 -> 0, of which waited for: 1 -> 0; matrix products, arithmetic and copies ran while one was open for 25% -> 0% of each run, Pallas kernels for 0% -> 0%
where the time goes in v2:
time: 58.9 us; the launch traced here: 58.7 us
  Pallas kernels  53.6 us (91%)
  local copies, waits for them, and re-layouts  4.49 us (8%)
  between operations  0.64 us (1%)
    pallas_call x1, Pallas kernels, dense_shards(): pl.pallas_call(fused_kernel, out_shape=(jax.ShapeDtypeStruct(block, full)...  53.6 us
    unnamed x3, local copies, waits for them, and re-layouts  4.49 us

profile of v2, /device:TPU:0, one launch (start us, length us, event | category | flops | bytes accessed | tf_op | source)
XLA Modules:
  0.0 58.7 jit_solution(16029175875420597455)
XLA Ops:
  0.6 53.6 %coadd_and_fit.1 = (f32[16,1024]{1,0:T(8,128)}, bf16[11,16,1024]{2,1,0:T(8,128)(2,1)}, f32[8,16]{1,0:T(8,128)}) custom-call(s32[32]{0:T(128)} %shift_s.1, s32[8,128]{1,0:T(8,128)} %bitcast.8, s32[8,128]{1,0:T(8,128)} %bitcast.9, f32[10,4608]{1,0:T(8,128)} %basis.1, bf16[128,1024]{1,0:T(8,128)(2,1)} %ivar_any.1, bf16[128,1024]{1,0:T(8,128)(2,1)} %flux_any.1, ...), custom_call_target="tpu_custom_call" | custom-call | tf_op jit(solution)/shard_map/coadd_and_fit/pallas_call | solution.py:430
  54.2 1.5 %copy.13 = f32[16,1024]{1,0:T(8,128)} copy(f32[16,1024]{1,0:T(8,128)} %get-tuple-element.12) | data formatting | bytes 131072
  55.7 1.7 %copy.14 = bf16[16,11,1024]{2,0,1:T(8,128)(2,1)} copy(bf16[16,11,1024]{2,0,1:T(8,128)(2,1)} %bitcast.6) | data formatting | bytes 720896
  57.4 1.3 %copy.15 = f32[16,8]{0,1:T(8,128)} copy(f32[16,8]{0,1:T(8,128)} %bitcast.7) | data formatting | bytes 1024

commit v3 on v2

--- a/solution.py
+++ b/solution.py
@@ -12,8 +12,10 @@
 NDIAG = 11
 Z_DEV = 8
 FIT_LANES = 256
-AHEAD = 3
-VMEM_LIMIT = 60 * 1024 * 1024
+AHEAD = 4
+ORDERS = ((0, 1, 2), (1, 0, 2))
+Z_FIRST = (1, 5, 9)
+VMEM_LIMIT = 52 * 1024 * 1024
 MESH = pl.DeviceIdType.MESH
 
 
@@ -188,27 +190,22 @@
 
 def fused_kernel(
     shift_s, target_v, valid_v, basis, ivar_any, flux_any, res_any,
-    flux_out, res_out, gain_out,
-    ivar, flux, res, weight, doubled, win,
-    sums_x, sums_in, sums_to, sums_z, sums_own,
-    res_x, res_in, res_to, res_z, res_own,
+    sums_out, res_out, gain_out,
+    ivar, flux, res, weight, member, win,
+    to_1, in_1, own_1, to_2, in_2, own_2, to_3, in_3, own_3,
     band_own, band_in, normal, right, inverse,
-    l_sem, x_send, x_recv, z_send, z_recv, b_send, b_recv,
+    l_sem, send_sem, recv_sem, b_send, b_recv,
 ):
     owners, rows = target_v.shape
     channels, wave_dev = res.shape[0], res.shape[-1]
+    pieces = channels + 2
     bands = lax.axis_size("band")
-    high_count = owners // 2
     waves = win.shape[2]
     basis_count = basis.shape[0]
     device = lax.axis_index("tgt")
     band = lax.axis_index("band")
-    high = device // 2
-    low = device % 2
-    partner = high * 2 + (1 - low)
-
-    def peer(d):
-        return lax.rem(high + d, high_count) * 2 + low
+    bits = [lax.rem(device // stride, 2) for stride in (1, 2, 4)]
+    partners = [device + (1 - 2 * bit) * stride for bit, stride in zip(bits, (1, 2, 4))]
 
     def band_peer(d):
         return lax.rem(band + d, bands)
@@ -223,8 +220,7 @@
         step.start()
 
     barrier = pltpu.get_barrier_semaphore()
-    near = [(partner, band)]
-    near += [(peer(d), band) for d in range(1, high_count)]
+    near = [(partner, band) for partner in partners]
     near += [(device, band_peer(d)) for d in range(1, bands)]
     for place in near:
         pl.semaphore_signal(barrier, inc=1, device_id=place, device_id_type=MESH)
@@ -235,93 +231,83 @@
             device_id=place, device_id_type=MESH,
         )
 
-    x_copies = [copy(sums_x, sums_in, x_send.at[0], x_recv.at[0], (partner, band))]
-    for k in range(channels):
-        x_copies.append(
-            copy(res_x.at[k], res_in.at[k], x_send.at[k + 1], x_recv.at[k + 1], (partner, band))
-        )
-    z_copies = []
-    for p in range(channels + 1):
-        row = []
-        for d in range(1, high_count):
-            source = sums_to.at[d - 1] if p == 0 else res_to.at[p - 1, d - 1]
-            target = sums_z.at[d - 1] if p == 0 else res_z.at[p - 1, d - 1]
-            row.append(
-                copy(source, target, z_send.at[p, d - 1], z_recv.at[p, d - 1], (peer(d), band))
+    def order_of(p):
+        return ORDERS[1] if p in Z_FIRST else ORDERS[0]
+
+    rounds = ((to_1, in_1), (to_2, in_2), (to_3, in_3))
+    copies = []
+    for p in range(pieces):
+        copies.append([
+            copy(
+                source.at[p], target.at[p], send_sem.at[p, r], recv_sem.at[p, r],
+                (partners[order_of(p)[r]], band),
             )
-        z_copies.append(row)
+            for r, (source, target) in enumerate(rounds)
+        ])
     b_copies = [
         copy(band_own, band_in.at[d - 1], b_send.at[d - 1], b_recv.at[d - 1], (device, band_peer(d)))
         for d in range(1, bands)
     ]
 
     count = owners * TGT_DEV
-    half = count // 2
     ids = lax.broadcasted_iota(jnp.int32, (count, rows), 0)
-    own_half = (ids >= half).astype(jnp.int32)
-    distance = (ids - own_half * half) // TGT_DEV
-    row_low = own_half * low + (1 - own_half) * (1 - low)
-    row_target = (lax.rem(distance + high, high_count) * 2 + row_low) * TGT_DEV + ids % TGT_DEV
     own_target = target_v[pl.ds(device, 1), :]
     own_valid = valid_v[pl.ds(device, 1), :]
-    member = jnp.where(row_target == own_target, own_valid, 0).astype(jnp.float32)
-    member = member.astype(jnp.bfloat16)
-    doubled[...] = jnp.concatenate([member, member], axis=1)
+    for which, order in enumerate(ORDERS):
+        owner = jnp.zeros_like(ids)
+        for r in range(3):
+            mine = (ids // (count >> (r + 1))) % 2
+            bit = mine * bits[order[r]] + (1 - mine) * (1 - bits[order[r]])
+            owner = owner + bit * (1 << order[r])
+        row_target = owner * TGT_DEV + ids % TGT_DEV
+        table = jnp.where(row_target == own_target, own_valid, 0).astype(jnp.float32)
+        table = table.astype(jnp.bfloat16)
+        member[which] = jnp.concatenate([table, table], axis=1)
     dims = (((1,), (0,)), ((), ()))
-
-    def summed(values):
-        product = weight[...] * values.astype(jnp.float32)
-        parts = jnp.concatenate(as_bf16_parts(product, 2), axis=0)
-        return lax.dot_general(doubled[...], parts, dims, preferred_element_type=jnp.float32)
-
-    def prepare_sums():
-        loads[0].wait()
-        loads[1].wait()
-        weight[...] = ivar[...].astype(jnp.float32)
-        for place, part in (
-            (0, lax.dot_general(member, ivar[...], dims, preferred_element_type=jnp.float32)),
-            (TGT_DEV, summed(flux[...])),
-        ):
-            for d in range(high_count):
-                span = slice(d * TGT_DEV, (d + 1) * TGT_DEV)
-                other = slice(half + d * TGT_DEV, half + (d + 1) * TGT_DEV)
-                sums_x[d, place : place + TGT_DEV, :] = part[span].astype(jnp.bfloat16)
-                sums_own[d, place : place + TGT_DEV, :] = part[other]
-
-    def prepare(k):
-        loads[k + 2].wait()
-        part = summed(res[k])
-        for d in range(high_count):
-            span = slice(d * TGT_DEV, (d + 1) * TGT_DEV)
-            other = slice(half + d * TGT_DEV, half + (d + 1) * TGT_DEV)
-            res_x[k, d] = part[span].astype(jnp.bfloat16)
-            res_own[k, d] = part[other]
-
-    def relay(p):
-        x_copies[p].wait_recv()
-        if p + AHEAD <= channels:
-            prepare(p + AHEAD - 1)
-            x_copies[p + AHEAD].start()
-        for d in range(1, high_count):
+    half, quarter, eighth = count // 2, count // 4, count // 8
+
+    def prepare(p):
+        loads[p].wait()
+        which = 1 if p in Z_FIRST else 0
+        if p == 0:
+            weight[...] = ivar[...].astype(jnp.float32)
+            part = lax.dot_general(
+                member[which, :, 0:rows], ivar[...], dims, preferred_element_type=jnp.float32
+            )
+        else:
+            values = flux[...] if p == 1 else res[p - 2]
+            product = weight[...] * values.astype(jnp.float32)
+            parts = jnp.concatenate(as_bf16_parts(product, 2), axis=0)
+            part = lax.dot_general(member[which], parts, dims, preferred_element_type=jnp.float32)
+        to_1[p] = part[0:half].astype(jnp.bfloat16)
+        own_1[p] = part[half:]
+
+    def round_1(p):
+        copies[p][0].wait_recv()
+        to_2[p] = (own_1[p, 0:quarter] + in_1[p, 0:quarter].astype(jnp.float32)).astype(jnp.bfloat16)
+        copies[p][1].start()
+        own_2[p] = own_1[p, quarter:] + in_1[p, quarter:].astype(jnp.float32)
+
+    def round_2(p):
+        copies[p][1].wait_recv()
+        to_3[p] = (own_2[p, 0:eighth] + in_2[p, 0:eighth].astype(jnp.float32)).astype(jnp.bfloat16)
+        copies[p][2].start()
+        own_3[p] = own_2[p, eighth:] + in_2[p, eighth:].astype(jnp.float32)
+
+    def round_3(p):
+        copies[p][2].wait_recv()
+        total = own_3[p] + in_3[p].astype(jnp.float32)
+        if p < 2:
+            sums_out[p] = total
+            band_own[p * TGT_DEV : (p + 1) * TGT_DEV, :] = total.astype(jnp.bfloat16)
             if p == 0:
-                total = sums_own[d] + sums_in[d].astype(jnp.float32)
-                sums_to[d - 1] = total.astype(jnp.bfloat16)
-            else:
-                total = res_own[p - 1, d] + res_in[p - 1, d].astype(jnp.float32)
-                res_to[p - 1, d - 1] = total.astype(jnp.bfloat16)
-            z_copies[p][d - 1].start()
-
-    def finish_sums():
-        total = sums_own[0] + sums_in[0].astype(jnp.float32)
-        for d in range(1, high_count):
-            z_copies[0][d - 1].wait_recv()
-            total = total + sums_z[d - 1].astype(jnp.float32)
-        band_own[...] = total.astype(jnp.bfloat16)
+                inverse[...] = 1.0 / total
+        else:
+            res_out[p - 2] = (total * inverse[...]).astype(jnp.bfloat16)
+
+    def send_sums():
         for step in b_copies:
             step.start()
-        weight_sum = total[0:TGT_DEV]
-        flux_out[...] = total[TGT_DEV:] / weight_sum
-        inverse[...] = 1.0 / weight_sum
 
     def make_windows(first, last):
         ids8 = lax.broadcasted_iota(jnp.int32, (Z_DEV, 128), 0)
@@ -375,38 +361,37 @@
         sides = [right[Z_DEV * b : Z_DEV * (b + 1), :] for b in range(basis_count)]
         gain_out[...] = solve_normal(matrix, jnp.stack(sides))
 
-    def finish(k):
-        total = res_own[k, 0] + res_in[k, 0].astype(jnp.float32)
-        for d in range(1, high_count):
-            z_copies[k + 1][d - 1].wait_recv()
-            total = total + res_z[k, d - 1].astype(jnp.float32)
-        res_out[k] = (total * inverse[...]).astype(jnp.bfloat16)
-
-    prepare_sums()
+    prepare(0)
+    prepare(1)
     pl.semaphore_wait(barrier, len(near))
-    x_copies[0].start()
-    for p in range(1, AHEAD):
-        prepare(p - 1)
-        x_copies[p].start()
+    copies[0][0].start()
+    copies[1][0].start()
+    for p in range(2, AHEAD):
+        prepare(p)
+        copies[p][0].start()
     jobs = [functools.partial(make_windows, 0, basis_count // 2)]
-    jobs += [functools.partial(make_windows, basis_count // 2, basis_count), finish_sums]
+    jobs += [functools.partial(make_windows, basis_count // 2, basis_count), send_sums]
     jobs += [functools.partial(fit_block, d) for d in range(bands)] + [solve]
-    relay(0)
-    finished = 0
-    for p in range(1, channels + 1):
-        relay(p)
-        if jobs:
+    for p in range(pieces + 3):
+        if p < pieces:
+            round_1(p)
+            if p + AHEAD < pieces:
+                prepare(p + AHEAD)
+                copies[p + AHEAD][0].start()
+        if 1 <= p <= pieces:
+            round_2(p - 1)
+        if p >= 3:
+            round_3(p - 3)
+        if p >= 2 and jobs:
             jobs.pop(0)()
-        if p >= 6:
-            finish(finished)
-            finished += 1
-    while jobs:
-        jobs.pop(0)()
-    while finished < channels:
-        finish(finished)
-        finished += 1
-    for step in x_copies + b_copies + [step for row in z_copies for step in row]:
+    for step in b_copies + [step for piece in copies for step in piece]:
         step.wait_send()
+
+
+def finish_kernel(sums, res, gain, flux_out, res_out, gain_out):
+    flux_out[...] = sums[1] / sums[0]
+    res_out[...] = res[...]
+    gain_out[...] = gain[...]
 
 
 def dense_shards(
@@ -417,20 +402,23 @@
     rows, wave_dev = exposure_flux.shape
     waves = wave_dev * bands
     basis_count = rest_basis.shape[0]
-    high_count = owners // 2
-    peers = high_count - 1
     pair_rows = Z_DEV * (len(pair_first) + 1)
     vmem = pl.BlockSpec(memory_space=pltpu.VMEM)
     smem = pl.BlockSpec(memory_space=pltpu.SMEM)
     hbm = pl.BlockSpec(memory_space=pl.ANY)
     half, full = jnp.bfloat16, jnp.float32
     block = (TGT_DEV, wave_dev)
-    sums = (2 * TGT_DEV, wave_dev)
+    count = owners * TGT_DEV
+    pieces = NDIAG + 2
+    buffers = []
+    for r in range(3):
+        shape = (pieces, count >> (r + 1), wave_dev)
+        buffers += [pltpu.VMEM(shape, half), pltpu.VMEM(shape, half), pltpu.VMEM(shape, full)]
     dma = pltpu.SemaphoreType.DMA
-    coadd_flux, coadd_res, gain = pl.pallas_call(
+    sums, coadd_res, gain = pl.pallas_call(
         fused_kernel,
         out_shape=(
-            jax.ShapeDtypeStruct(block, full),
+            jax.ShapeDtypeStruct((2,) + block, full),
             jax.ShapeDtypeStruct((NDIAG,) + block, half),
             jax.ShapeDtypeStruct((Z_DEV, TGT_DEV), full),
         ),
@@ -441,28 +429,17 @@
             pltpu.VMEM((rows, wave_dev), half),
             pltpu.VMEM((NDIAG, rows, wave_dev), half),
             pltpu.VMEM((rows, wave_dev), full),
-            pltpu.VMEM((owners * TGT_DEV, 2 * rows), half),
+            pltpu.VMEM((2, count, 2 * rows), half),
             pltpu.VMEM((basis_count, Z_DEV, waves), full),
-            pltpu.VMEM((high_count,) + sums, half),
-            pltpu.VMEM((high_count,) + sums, half),
-            pltpu.VMEM((peers,) + sums, half),
-            pltpu.VMEM((peers,) + sums, half),
-            pltpu.VMEM((high_count,) + sums, full),
-            pltpu.VMEM((NDIAG, high_count) + block, half),
-            pltpu.VMEM((NDIAG, high_count) + block, half),
-            pltpu.VMEM((NDIAG, peers) + block, half),
-            pltpu.VMEM((NDIAG, peers) + block, half),
-            pltpu.VMEM((NDIAG, high_count) + block, full),
-            pltpu.VMEM(sums, half),
-            pltpu.VMEM((bands - 1,) + sums, half),
+        ] + buffers + [
+            pltpu.VMEM((2 * TGT_DEV, wave_dev), half),
+            pltpu.VMEM((bands - 1, 2 * TGT_DEV, wave_dev), half),
             pltpu.VMEM((pair_rows, TGT_DEV), full),
             pltpu.VMEM((Z_DEV * basis_count, TGT_DEV), full),
             pltpu.VMEM(block, full),
-            dma((NDIAG + 2,)),
-            dma((NDIAG + 1,)),
-            dma((NDIAG + 1,)),
-            dma((NDIAG + 1, peers)),
-            dma((NDIAG + 1, peers)),
+            dma((pieces,)),
+            dma((pieces, 3)),
+            dma((pieces, 3)),
             dma((bands - 1,)),
             dma((bands - 1,)),
         ],
@@ -475,6 +452,17 @@
         target_of_row.reshape(owners, rows), valid_of_row.reshape(owners, rows), rest_basis,
         exposure_ivar, exposure_flux, jnp.transpose(exposure_res, (1, 0, 2)),
     )
+    coadd_flux, coadd_res, gain = pl.pallas_call(
+        finish_kernel,
+        out_shape=(
+            jax.ShapeDtypeStruct(block, full),
+            jax.ShapeDtypeStruct(coadd_res.shape, half),
+            jax.ShapeDtypeStruct(gain.shape, full),
+        ),
+        in_specs=[vmem] * 3,
+        out_specs=(vmem, vmem, vmem),
+        name="finish",
+    )(sums, coadd_res, gain)
     return (coadd_flux, jnp.transpose(coadd_res, (1, 0, 2)), gain.T)
 
 
@@ -485,7 +473,7 @@
 
     def whole(*args):
         rows = args[0].shape[0] // owners
-        body = dense_shards if owners * TGT_DEV <= 2 * rows and owners % 2 == 0 else shards
+        body = dense_shards if owners * TGT_DEV <= 2 * rows and owners == 8 else shards
         return jax.shard_map(
             body, mesh=mesh, in_specs=in_specs, out_specs=out_specs, check_vma=False
         )(*args)

time: 58.9 us -> 62.6 us (1.063)
  local copies, waits for them, and re-layouts: 4.49 us -> 6.85 us
  Pallas kernels: 53.6 us -> 54.8 us
    unnamed x3 -> x18, local copies, waits for them, and re-layouts: 4.49 us -> 6.85 us
    pallas_call x1 -> x2, Pallas kernels: 53.6 us -> 54.8 us  [the longest x1 53 us: dense_shards(): pl.pallas_call(fused_kernel, out_shape=(jax.ShapeDtypeStruct((2,) + block...]
where the time goes in v3:
time: 62.6 us; the launch traced here: 62.3 us
  Pallas kernels  54.8 us (88%)
  local copies, waits for them, and re-layouts  6.85 us (11%)
  between operations  0.66 us (1%)
    pallas_call x1, Pallas kernels, dense_shards(): pl.pallas_call(fused_kernel, out_shape=(jax.ShapeDtypeStruct((2,) + block...  53 us
    unnamed x18, local copies, waits for them, and re-layouts  6.85 us
    pallas_call x1, Pallas kernels, dense_shards(): pl.pallas_call(finish_kernel, out_shape=(jax.ShapeDtypeStruct(block, full...  1.79 us

profile of v3, /device:TPU:0, one launch (start us, length us, event | category | flops | bytes accessed | tf_op | source)
XLA Modules:
  0.0 62.3 jit_solution(6588519029205619376)
XLA Ops:
  0.6 0.0 copy-start.1
  0.6 1.0 %copy-done.1 = f32[10,4608]{1,0:T(8,128)S(1)} copy-done((f32[10,4608]{1,0:T(8,128)S(1)}, f32[10,4608]{1,0:T(8,128)}, u32[]{:S(2)}) %copy-start.1) | copy-done | bytes 184344
  1.6 0.0 copy-start.2
  1.6 0.9 %copy-done.2 = bf16[128,1024]{1,0:T(8,128)(2,1)S(1)} copy-done((bf16[128,1024]{1,0:T(8,128)(2,1)S(1)}, bf16[128,1024]{1,0:T(8,128)(2,1)}, u32[]{:S(2)}) %copy-start.2) | copy-done | bytes 262168
  2.5 0.0 copy-start.3
  2.5 0.9 %copy-done.3 = bf16[128,1024]{1,0:T(8,128)(2,1)S(1)} copy-done((bf16[128,1024]{1,0:T(8,128)(2,1)S(1)}, bf16[128,1024]{1,0:T(8,128)(2,1)}, u32[]{:S(2)}) %copy-start.3) | copy-done | bytes 262168
  3.5 0.0 copy-start.6
  3.5 0.7 %copy-done.6 = s32[1024]{0:T(1024)S(1)} copy-done((s32[1024]{0:T(1024)S(1)}, s32[1024]{0:T(1024)}, u32[]{:S(2)}) %copy-start.6) | copy-done | bytes 4120
  4.2 0.0 copy-start.7
  4.2 0.7 %copy-done.7 = s32[1024]{0:T(1024)S(1)} copy-done((s32[1024]{0:T(1024)S(1)}, s32[1024]{0:T(1024)}, u32[]{:S(2)}) %copy-start.7) | copy-done | bytes 4120
  4.9 0.0 copy-start.8
  4.9 0.7 %copy-done.8 = s32[32]{0:T(128)S(1)} copy-done((s32[32]{0:T(128)S(1)}, s32[32]{0:T(128)}, u32[]{:S(2)}) %copy-start.8) | copy-done | bytes 152
  5.5 53.0 %coadd_and_fit.1 = (f32[2,16,1024]{2,1,0:T(8,128)S(1)}, bf16[11,16,1024]{2,1,0:T(8,128)(2,1)S(1)}, f32[8,16]{1,0:T(8,128)S(1)}) custom-call(s32[32]{0:T(128)S(1)} %copy-done.8, s32[8,128]{1,0:T(8,128)S(1)} %bitcast.5, s32[8,128]{1,0:T(8,128)S(1)} %bitcast.6, f32[10,4608]{1,0:T(8,128)S(1)} %copy-done.1, bf16[128,1024]{1,0:T(8,128)(2,1)S(1)} %copy-done.2, ...), custom_call_target="tpu_custom_call" | custom-call | tf_op jit(solution)/shard_map/coadd_and_fit/pallas_call | solution.py:418
  58.6 0.0 copy-start
  58.6 0.7 %copy-done = bf16[11,16,1024]{2,1,0:T(8,128)(2,1)} copy-done((bf16[11,16,1024]{2,1,0:T(8,128)(2,1)}, bf16[11,16,1024]{2,1,0:T(8,128)(2,1)S(1)}, u32[]{:S(2)}) %copy-start) | copy-done | bytes 360472
  59.3 0.0 copy-start.4
  59.3 0.7 %copy-done.4 = f32[2,16,1024]{2,1,0:T(8,128)} copy-done((f32[2,16,1024]{2,1,0:T(8,128)}, f32[2,16,1024]{2,1,0:T(8,128)S(1)}, u32[]{:S(2)}) %copy-start.4) | copy-done | bytes 131096
  59.9 0.0 copy-start.5
  59.9 0.6 copy-done.5
  60.5 1.8 %finish.1 = (f32[16,1024]{1,0:T(8,128)}, bf16[11,16,1024]{2,1,0:T(8,128)(2,1)}, f32[8,16]{1,0:T(8,128)}) custom-call(f32[2,16,1024]{2,1,0:T(8,128)} %copy-done.4, bf16[11,16,1024]{2,1,0:T(8,128)(2,1)} %copy-done, f32[8,16]{1,0:T(8,128)} %copy-done.5), custom_call_target="tpu_custom_call" | custom-call | tf_op jit(solution)/shard_map/finish/pallas_call | solution.py:455
Async XLA Ops:
  0.6 1.0 %copy-start.1 = (f32[10,4608]{1,0:T(8,128)S(1)}, f32[10,4608]{1,0:T(8,128)}, u32[]{:S(2)}) copy-start(f32[10,4608]{1,0:T(8,128)} %basis.1) | copy-start | bytes 552964
  1.6 0.9 %copy-start.2 = (bf16[128,1024]{1,0:T(8,128)(2,1)S(1)}, bf16[128,1024]{1,0:T(8,128)(2,1)}, u32[]{:S(2)}) copy-start(bf16[128,1024]{1,0:T(8,128)(2,1)} %ivar_any.1) | copy-start | bytes 786436
  2.5 0.9 %copy-start.3 = (bf16[128,1024]{1,0:T(8,128)(2,1)S(1)}, bf16[128,1024]{1,0:T(8,128)(2,1)}, u32[]{:S(2)}) copy-start(bf16[128,1024]{1,0:T(8,128)(2,1)} %flux_any.1) | copy-start | bytes 786436
  3.5 0.7 %copy-start.6 = (s32[1024]{0:T(1024)S(1)}, s32[1024]{0:T(1024)}, u32[]{:S(2)}) copy-start(s32[1024]{0:T(1024)} %param.10) | copy-start | bytes 12292
  4.2 0.7 %copy-start.7 = (s32[1024]{0:T(1024)S(1)}, s32[1024]{0:T(1024)}, u32[]{:S(2)}) copy-start(s32[1024]{0:T(1024)} %param.11) | copy-start | bytes 12292
  4.9 0.7 %copy-start.8 = (s32[32]{0:T(128)S(1)}, s32[32]{0:T(128)}, u32[]{:S(2)}) copy-start(s32[32]{0:T(128)} %shift_s.1) | copy-start | bytes 388
  58.6 0.7 %copy-start = (bf16[11,16,1024]{2,1,0:T(8,128)(2,1)}, bf16[11,16,1024]{2,1,0:T(8,128)(2,1)S(1)}, u32[]{:S(2)}) copy-start(bf16[11,16,1024]{2,1,0:T(8,128)(2,1)S(1)} %get-tuple-element.10.res) | copy-start | bytes 1081348
  59.3 0.7 %copy-start.4 = (f32[2,16,1024]{2,1,0:T(8,128)}, f32[2,16,1024]{2,1,0:T(8,128)S(1)}, u32[]{:S(2)}) copy-start(f32[2,16,1024]{2,1,0:T(8,128)S(1)} %get-tuple-element.9.sums) | copy-start | bytes 393220
  59.9 0.6 copy-start.5

commit v4 on v3

--- a/solution.py
+++ b/solution.py
@@ -12,10 +12,11 @@
 NDIAG = 11
 Z_DEV = 8
 FIT_LANES = 256
-AHEAD = 4
+AHEAD = 6
+FIT_PARTS = 2
 ORDERS = ((0, 1, 2), (1, 0, 2))
 Z_FIRST = (1, 5, 9)
-VMEM_LIMIT = 52 * 1024 * 1024
+VMEM_LIMIT = 60 * 1024 * 1024
 MESH = pl.DeviceIdType.MESH
 
 
@@ -190,11 +191,11 @@
 
 def fused_kernel(
     shift_s, target_v, valid_v, basis, ivar_any, flux_any, res_any,
-    sums_out, res_out, gain_out,
+    flux_out, res_out, gain_out,
     ivar, flux, res, weight, member, win,
     to_1, in_1, own_1, to_2, in_2, own_2, to_3, in_3, own_3,
-    band_own, band_in, normal, right, inverse,
-    l_sem, send_sem, recv_sem, b_send, b_recv,
+    band_own, band_in, normal, right, inverse, res_done,
+    l_sem, o_sem, send_sem, recv_sem, b_send, b_recv,
 ):
     owners, rows = target_v.shape
     channels, wave_dev = res.shape[0], res.shape[-1]
@@ -219,6 +220,9 @@
     for step in loads:
         step.start()
 
+    stores = [
+        pltpu.make_async_copy(res_done.at[k], res_out.at[k], o_sem.at[k]) for k in range(channels)
+    ]
     barrier = pltpu.get_barrier_semaphore()
     near = [(partner, band) for partner in partners]
     near += [(device, band_peer(d)) for d in range(1, bands)]
@@ -253,7 +257,9 @@
     ids = lax.broadcasted_iota(jnp.int32, (count, rows), 0)
     own_target = target_v[pl.ds(device, 1), :]
     own_valid = valid_v[pl.ds(device, 1), :]
-    for which, order in enumerate(ORDERS):
+
+    def make_member(which):
+        order = ORDERS[which]
         owner = jnp.zeros_like(ids)
         for r in range(3):
             mine = (ids // (count >> (r + 1))) % 2
@@ -298,12 +304,14 @@
         copies[p][2].wait_recv()
         total = own_3[p] + in_3[p].astype(jnp.float32)
         if p < 2:
-            sums_out[p] = total
             band_own[p * TGT_DEV : (p + 1) * TGT_DEV, :] = total.astype(jnp.bfloat16)
             if p == 0:
                 inverse[...] = 1.0 / total
+            else:
+                flux_out[...] = total * inverse[...]
         else:
-            res_out[p - 2] = (total * inverse[...]).astype(jnp.bfloat16)
+            res_done[p - 2] = (total * inverse[...]).astype(jnp.bfloat16)
+            stores[p - 2].start()
 
     def send_sums():
         for step in b_copies:
@@ -334,21 +342,23 @@
 
         lax.fori_loop(first, last, one_basis, 0)
 
-    def fit_block(d):
+    def fit_block(d, part):
         if d == 0:
             source, place = band_own, band
         else:
-            b_copies[d - 1].wait_recv()
+            if part == 0:
+                b_copies[d - 1].wait_recv()
             source, place = band_in.at[d - 1], lax.rem(band + (bands - d), bands)
         last = ((1,), (1,))
-        for step in range(wave_dev // FIT_LANES):
+        steps = wave_dev // FIT_LANES // 2
+        for step in range(part * steps, (part + 1) * steps):
             span = slice(step * FIT_LANES, (step + 1) * FIT_LANES)
             at = pl.multiple_of(place * wave_dev + step * FIT_LANES, FIT_LANES)
             bases = [win[b, :, pl.ds(at, FIT_LANES)] for b in range(basis_count)]
             pairs = [bases[int(b)] * bases[int(c)] for b, c in zip(pair_first, pair_second)]
             pairs.append(pairs[0])
-            matrix = exact_dot(jnp.concatenate(pairs, axis=0), source[0:TGT_DEV, span], last, 3)
-            sides = exact_dot(jnp.concatenate(bases, axis=0), source[TGT_DEV:, span], last, 3)
+            matrix = exact_dot(jnp.concatenate(pairs, axis=0), source[0:TGT_DEV, span], last, FIT_PARTS)
+            sides = exact_dot(jnp.concatenate(bases, axis=0), source[TGT_DEV:, span], last, FIT_PARTS)
             if d == 0 and step == 0:
                 normal[...] = matrix
                 right[...] = sides
@@ -361,17 +371,19 @@
         sides = [right[Z_DEV * b : Z_DEV * (b + 1), :] for b in range(basis_count)]
         gain_out[...] = solve_normal(matrix, jnp.stack(sides))
 
+    make_member(0)
     prepare(0)
-    prepare(1)
     pl.semaphore_wait(barrier, len(near))
     copies[0][0].start()
-    copies[1][0].start()
-    for p in range(2, AHEAD):
+    make_member(1)
+    for p in range(1, AHEAD):
         prepare(p)
         copies[p][0].start()
-    jobs = [functools.partial(make_windows, 0, basis_count // 2)]
-    jobs += [functools.partial(make_windows, basis_count // 2, basis_count), send_sums]
-    jobs += [functools.partial(fit_block, d) for d in range(bands)] + [solve]
+    middle = basis_count // 2
+    jobs = [
+        functools.partial(make_windows, 0, middle), functools.partial(make_windows, middle, basis_count)
+    ]
+    jobs += [send_sums] + [functools.partial(fit_block, d, h) for d in range(bands) for h in range(2)] + [solve]
     for p in range(pieces + 3):
         if p < pieces:
             round_1(p)
@@ -382,16 +394,25 @@
             round_2(p - 1)
         if p >= 3:
             round_3(p - 3)
-        if p >= 2 and jobs:
-            jobs.pop(0)()
+        for repeat in range((0, 1, 1, 0, 2, 2, 2)[p] if p < 7 else 1):
+            if jobs:
+                jobs.pop(0)()
     for step in b_copies + [step for piece in copies for step in piece]:
         step.wait_send()
-
-
-def finish_kernel(sums, res, gain, flux_out, res_out, gain_out):
-    flux_out[...] = sums[1] / sums[0]
-    res_out[...] = res[...]
-    gain_out[...] = gain[...]
+    for step in stores:
+        step.wait()
+
+
+def finish_kernel(flux, res, gain, flux_out, res_out, gain_out, sem):
+    steps = [
+        pltpu.make_async_copy(res, res_out, sem.at[0]),
+        pltpu.make_async_copy(flux, flux_out, sem.at[1]),
+        pltpu.make_async_copy(gain, gain_out, sem.at[2]),
+    ]
+    for step in steps:
+        step.start()
+    for step in steps:
+        step.wait()
 
 
 def dense_shards(
@@ -415,15 +436,15 @@
         shape = (pieces, count >> (r + 1), wave_dev)
         buffers += [pltpu.VMEM(shape, half), pltpu.VMEM(shape, half), pltpu.VMEM(shape, full)]
     dma = pltpu.SemaphoreType.DMA
-    sums, coadd_res, gain = pl.pallas_call(
+    coadd_flux, coadd_res, gain = pl.pallas_call(
         fused_kernel,
         out_shape=(
-            jax.ShapeDtypeStruct((2,) + block, full),
+            jax.ShapeDtypeStruct(block, full),
             jax.ShapeDtypeStruct((NDIAG,) + block, half),
             jax.ShapeDtypeStruct((Z_DEV, TGT_DEV), full),
         ),
         in_specs=[smem, vmem, vmem, vmem, hbm, hbm, hbm],
-        out_specs=(vmem, vmem, vmem),
+        out_specs=(vmem, hbm, vmem),
         scratch_shapes=[
             pltpu.VMEM((rows, wave_dev), half),
             pltpu.VMEM((rows, wave_dev), half),
@@ -437,7 +458,9 @@
             pltpu.VMEM((pair_rows, TGT_DEV), full),
             pltpu.VMEM((Z_DEV * basis_count, TGT_DEV), full),
             pltpu.VMEM(block, full),
+            pltpu.VMEM((NDIAG,) + block, half),
             dma((pieces,)),
+            dma((NDIAG,)),
             dma((pieces, 3)),
             dma((pieces, 3)),
             dma((bands - 1,)),
@@ -459,10 +482,12 @@
             jax.ShapeDtypeStruct(coadd_res.shape, half),
             jax.ShapeDtypeStruct(gain.shape, full),
         ),
-        in_specs=[vmem] * 3,
-        out_specs=(vmem, vmem, vmem),
+        in_specs=[hbm] * 3,
+        out_specs=(hbm, hbm, hbm),
+        scratch_shapes=[dma((3,))],
+        compiler_params=pltpu.CompilerParams(vmem_limit_bytes=VMEM_LIMIT),
         name="finish",
-    )(sums, coadd_res, gain)
+    )(coadd_flux, coadd_res, gain)
     return (coadd_flux, jnp.transpose(coadd_res, (1, 0, 2)), gain.T)
 
 

time: 62.6 us -> 73.1 us (1.17)
  Pallas kernels: 54.8 us -> 72.3 us
  local copies, waits for them, and re-layouts: 6.85 us -> 0 us
    pallas_call x1, Pallas kernels: 1.79 us -> 14.2 us  [dense_shards(): pl.pallas_call(finish_kernel, out_shape=(jax.ShapeDtypeStruct(block, full...]
    unnamed x18 -> x0, local copies, waits for them, and re-layouts: 6.85 us -> none
    pallas_call x1, Pallas kernels: 53 us -> 58.1 us  [dense_shards(): pl.pallas_call(fused_kernel, out_shape=(jax.ShapeDtypeStruct(block, full)...]
where the time goes in v4:
time: 73.1 us; the launch traced here: 72.9 us
  Pallas kernels  72.3 us (99%)
    pallas_call x1, Pallas kernels, dense_shards(): pl.pallas_call(fused_kernel, out_shape=(jax.ShapeDtypeStruct(block, full)...  58.1 us
    pallas_call x1, Pallas kernels, dense_shards(): pl.pallas_call(finish_kernel, out_shape=(jax.ShapeDtypeStruct(block, full...  14.2 us

profile of v4, /device:TPU:0, one launch (start us, length us, event | category | flops | bytes accessed | tf_op | source)
XLA Modules:
  0.0 72.9 jit_solution(2734414684126292131)
XLA Ops:
  0.6 58.1 %coadd_and_fit.1 = (f32[16,1024]{1,0:T(8,128)}, bf16[11,16,1024]{2,1,0:T(8,128)(2,1)}, f32[8,16]{1,0:T(8,128)}) custom-call(s32[32]{0:T(128)} %shift_s.1, s32[8,128]{1,0:T(8,128)} %bitcast.6, s32[8,128]{1,0:T(8,128)} %bitcast.7, f32[10,4608]{1,0:T(8,128)} %basis.1, bf16[128,1024]{1,0:T(8,128)(2,1)} %ivar_any.1, bf16[128,1024]{1,0:T(8,128)(2,1)} %flux_any.1, ...), custom_call_target="tpu_custom_call" | custom-call | tf_op jit(solution)/shard_map/coadd_and_fit/pallas_call | solution.py:439
  58.8 14.2 %finish.1 = (f32[16,1024]{1,0:T(8,128)}, bf16[11,16,1024]{2,1,0:T(8,128)(2,1)}, f32[8,16]{1,0:T(8,128)}) custom-call(f32[16,1024]{1,0:T(8,128)} %get-tuple-element.9.flux, bf16[11,16,1024]{2,1,0:T(8,128)(2,1)} %get-tuple-element.10.res, f32[8,16]{1,0:T(8,128)} %get-tuple-element.11.gain), custom_call_target="tpu_custom_call" | custom-call | tf_op jit(solution)/shard_map/finish/pallas_call | solution.py:478

commit v5 on v4

--- a/solution.py
+++ b/solution.py
@@ -12,10 +12,10 @@
 NDIAG = 11
 Z_DEV = 8
 FIT_LANES = 256
-AHEAD = 6
+AHEAD = 3
 FIT_PARTS = 2
 ORDERS = ((0, 1, 2), (1, 0, 2))
-Z_FIRST = (1, 5, 9)
+Z_FIRST = ((2, 6, 10), (0, 4, 8))
 VMEM_LIMIT = 60 * 1024 * 1024
 MESH = pl.DeviceIdType.MESH
 
@@ -194,8 +194,8 @@
     flux_out, res_out, gain_out,
     ivar, flux, res, weight, member, win,
     to_1, in_1, own_1, to_2, in_2, own_2, to_3, in_3, own_3,
-    band_own, band_in, normal, right, inverse, res_done,
-    l_sem, o_sem, send_sem, recv_sem, b_send, b_recv,
+    band_own, band_in, normal, right, inverse,
+    l_sem, send_sem, recv_sem, b_send, b_recv,
 ):
     owners, rows = target_v.shape
     channels, wave_dev = res.shape[0], res.shape[-1]
@@ -220,9 +220,6 @@
     for step in loads:
         step.start()
 
-    stores = [
-        pltpu.make_async_copy(res_done.at[k], res_out.at[k], o_sem.at[k]) for k in range(channels)
-    ]
     barrier = pltpu.get_barrier_semaphore()
     near = [(partner, band) for partner in partners]
     near += [(device, band_peer(d)) for d in range(1, bands)]
@@ -235,8 +232,17 @@
             device_id=place, device_id_type=MESH,
         )
 
+    core = lax.rem(band, 2)
+
     def order_of(p):
-        return ORDERS[1] if p in Z_FIRST else ORDERS[0]
+        if p in Z_FIRST[0]:
+            return 1 - core
+        return core if p in Z_FIRST[1] else 0
+
+    def partner_of(p, r):
+        which = order_of(p)
+        first, second = partners[ORDERS[0][r]], partners[ORDERS[1][r]]
+        return (1 - which) * first + which * second
 
     rounds = ((to_1, in_1), (to_2, in_2), (to_3, in_3))
     copies = []
@@ -244,7 +250,7 @@
         copies.append([
             copy(
                 source.at[p], target.at[p], send_sem.at[p, r], recv_sem.at[p, r],
-                (partners[order_of(p)[r]], band),
+                (partner_of(p, r), band),
             )
             for r, (source, target) in enumerate(rounds)
         ])
@@ -274,7 +280,7 @@
 
     def prepare(p):
         loads[p].wait()
-        which = 1 if p in Z_FIRST else 0
+        which = order_of(p)
         if p == 0:
             weight[...] = ivar[...].astype(jnp.float32)
             part = lax.dot_general(
@@ -290,6 +296,8 @@
 
     def round_1(p):
         copies[p][0].wait_recv()
+        if p + AHEAD < pieces:
+            copies[p + AHEAD][0].start()
         to_2[p] = (own_1[p, 0:quarter] + in_1[p, 0:quarter].astype(jnp.float32)).astype(jnp.bfloat16)
         copies[p][1].start()
         own_2[p] = own_1[p, quarter:] + in_1[p, quarter:].astype(jnp.float32)
@@ -310,8 +318,7 @@
             else:
                 flux_out[...] = total * inverse[...]
         else:
-            res_done[p - 2] = (total * inverse[...]).astype(jnp.bfloat16)
-            stores[p - 2].start()
+            res_out[p - 2] = (total * inverse[...]).astype(jnp.bfloat16)
 
     def send_sums():
         for step in b_copies:
@@ -372,13 +379,14 @@
         gain_out[...] = solve_normal(matrix, jnp.stack(sides))
 
     make_member(0)
+    make_member(1)
     prepare(0)
     pl.semaphore_wait(barrier, len(near))
     copies[0][0].start()
-    make_member(1)
     for p in range(1, AHEAD):
         prepare(p)
         copies[p][0].start()
+    prepare(AHEAD)
     middle = basis_count // 2
     jobs = [
         functools.partial(make_windows, 0, middle), functools.partial(make_windows, middle, basis_count)
@@ -387,9 +395,8 @@
     for p in range(pieces + 3):
         if p < pieces:
             round_1(p)
-            if p + AHEAD < pieces:
-                prepare(p + AHEAD)
-                copies[p + AHEAD][0].start()
+            if p + AHEAD + 1 < pieces:
+                prepare(p + AHEAD + 1)
         if 1 <= p <= pieces:
             round_2(p - 1)
         if p >= 3:
@@ -399,20 +406,12 @@
                 jobs.pop(0)()
     for step in b_copies + [step for piece in copies for step in piece]:
         step.wait_send()
-    for step in stores:
-        step.wait()
-
-
-def finish_kernel(flux, res, gain, flux_out, res_out, gain_out, sem):
-    steps = [
-        pltpu.make_async_copy(res, res_out, sem.at[0]),
-        pltpu.make_async_copy(flux, flux_out, sem.at[1]),
-        pltpu.make_async_copy(gain, gain_out, sem.at[2]),
-    ]
-    for step in steps:
-        step.start()
-    for step in steps:
-        step.wait()
+
+
+def finish_kernel(flux, res, gain, flux_out, res_out, gain_out):
+    flux_out[...] = flux[...]
+    res_out[...] = res[...]
+    gain_out[...] = gain[...]
 
 
 def dense_shards(
@@ -444,7 +443,7 @@
             jax.ShapeDtypeStruct((Z_DEV, TGT_DEV), full),
         ),
         in_specs=[smem, vmem, vmem, vmem, hbm, hbm, hbm],
-        out_specs=(vmem, hbm, vmem),
+        out_specs=(vmem, vmem, vmem),
         scratch_shapes=[
             pltpu.VMEM((rows, wave_dev), half),
             pltpu.VMEM((rows, wave_dev), half),
@@ -458,9 +457,7 @@
             pltpu.VMEM((pair_rows, TGT_DEV), full),
             pltpu.VMEM((Z_DEV * basis_count, TGT_DEV), full),
             pltpu.VMEM(block, full),
-            pltpu.VMEM((NDIAG,) + block, half),
             dma((pieces,)),
-            dma((NDIAG,)),
             dma((pieces, 3)),
             dma((pieces, 3)),
             dma((bands - 1,)),
@@ -482,9 +479,8 @@
             jax.ShapeDtypeStruct(coadd_res.shape, half),
             jax.ShapeDtypeStruct(gain.shape, full),
         ),
-        in_specs=[hbm] * 3,
-        out_specs=(hbm, hbm, hbm),
-        scratch_shapes=[dma((3,))],
+        in_specs=[vmem] * 3,
+        out_specs=(vmem, vmem, vmem),
         compiler_params=pltpu.CompilerParams(vmem_limit_bytes=VMEM_LIMIT),
         name="finish",
     )(coadd_flux, coadd_res, gain)

time: 73.1 us -> 56.7 us (0.78)
  Pallas kernels: 72.3 us -> 55.9 us
    pallas_call x1, Pallas kernels: 14.2 us -> 1.76 us  [dense_shards(): pl.pallas_call(finish_kernel, out_shape=(jax.ShapeDtypeStruct(block, full...]
    pallas_call x1, Pallas kernels: 58.1 us -> 54.2 us  [dense_shards(): pl.pallas_call(fused_kernel, out_shape=(jax.ShapeDtypeStruct(block, full)...]
where the time goes in v5:
time: 56.7 us; the launch traced here: 56.6 us
  Pallas kernels  55.9 us (99%)
  between operations  0.64 us (1%)
    pallas_call x1, Pallas kernels, dense_shards(): pl.pallas_call(fused_kernel, out_shape=(jax.ShapeDtypeStruct(block, full)...  54.2 us
    pallas_call x1, Pallas kernels, dense_shards(): pl.pallas_call(finish_kernel, out_shape=(jax.ShapeDtypeStruct(block, full...  1.76 us

profile of v5, /device:TPU:0, one launch (start us, length us, event | category | flops | bytes accessed | tf_op | source)
XLA Modules:
  0.0 56.6 jit_solution(12657281283880045825)
XLA Ops:
  0.6 54.2 %coadd_and_fit.1 = (f32[16,1024]{1,0:T(8,128)}, bf16[11,16,1024]{2,1,0:T(8,128)(2,1)}, f32[8,16]{1,0:T(8,128)}) custom-call(s32[32]{0:T(128)} %shift_s.1, s32[8,128]{1,0:T(8,128)} %bitcast.6, s32[8,128]{1,0:T(8,128)} %bitcast.7, f32[10,4608]{1,0:T(8,128)} %basis.1, bf16[128,1024]{1,0:T(8,128)(2,1)} %ivar_any.1, bf16[128,1024]{1,0:T(8,128)(2,1)} %flux_any.1, ...), custom_call_target="tpu_custom_call" | custom-call | tf_op jit(solution)/shard_map/coadd_and_fit/pallas_call | solution.py:438
  54.8 1.8 %finish.1 = (f32[16,1024]{1,0:T(8,128)}, bf16[11,16,1024]{2,1,0:T(8,128)(2,1)}, f32[8,16]{1,0:T(8,128)}) custom-call(f32[16,1024]{1,0:T(8,128)} %get-tuple-element.9.flux, bf16[11,16,1024]{2,1,0:T(8,128)(2,1)} %get-tuple-element.10.res, f32[8,16]{1,0:T(8,128)} %get-tuple-element.11.gain), custom_call_target="tpu_custom_call" | custom-call | tf_op jit(solution)/shard_map/finish/pallas_call | solution.py:475

commit v6 on v5

--- a/solution.py
+++ b/solution.py
@@ -12,7 +12,7 @@
 NDIAG = 11
 Z_DEV = 8
 FIT_LANES = 256
-AHEAD = 3
+AHEAD = 2
 FIT_PARTS = 2
 ORDERS = ((0, 1, 2), (1, 0, 2))
 Z_FIRST = ((2, 6, 10), (0, 4, 8))

time: 56.7 us -> 58.1 us (1.025)
  Pallas kernels: 55.9 us -> 57.3 us
    pallas_call x1, Pallas kernels: 54.2 us -> 55.5 us  [dense_shards(): pl.pallas_call(fused_kernel, out_shape=(jax.ShapeDtypeStruct(block, full)...]
where the time goes in v6:
time: 58.1 us; the launch traced here: 57.9 us
  Pallas kernels  57.3 us (99%)
  between operations  0.64 us (1%)
    pallas_call x1, Pallas kernels, dense_shards(): pl.pallas_call(fused_kernel, out_shape=(jax.ShapeDtypeStruct(block, full)...  55.5 us
    pallas_call x1, Pallas kernels, dense_shards(): pl.pallas_call(finish_kernel, out_shape=(jax.ShapeDtypeStruct(block, full...  1.76 us

profile of v6, /device:TPU:0, one launch (start us, length us, event | category | flops | bytes accessed | tf_op | source)
XLA Modules:
  0.0 57.9 jit_solution(5247868679758870901)
XLA Ops:
  0.6 55.5 %coadd_and_fit.1 = (f32[16,1024]{1,0:T(8,128)}, bf16[11,16,1024]{2,1,0:T(8,128)(2,1)}, f32[8,16]{1,0:T(8,128)}) custom-call(s32[32]{0:T(128)} %shift_s.1, s32[8,128]{1,0:T(8,128)} %bitcast.6, s32[8,128]{1,0:T(8,128)} %bitcast.7, f32[10,4608]{1,0:T(8,128)} %basis.1, bf16[128,1024]{1,0:T(8,128)(2,1)} %ivar_any.1, bf16[128,1024]{1,0:T(8,128)(2,1)} %flux_any.1, ...), custom_call_target="tpu_custom_call" | custom-call | tf_op jit(solution)/shard_map/coadd_and_fit/pallas_call | solution.py:438
  56.2 1.8 %finish.1 = (f32[16,1024]{1,0:T(8,128)}, bf16[11,16,1024]{2,1,0:T(8,128)(2,1)}, f32[8,16]{1,0:T(8,128)}) custom-call(f32[16,1024]{1,0:T(8,128)} %get-tuple-element.9.flux, bf16[11,16,1024]{2,1,0:T(8,128)(2,1)} %get-tuple-element.10.res, f32[8,16]{1,0:T(8,128)} %get-tuple-element.11.gain), custom_call_target="tpu_custom_call" | custom-call | tf_op jit(solution)/shard_map/finish/pallas_call | solution.py:475
